TPU v7x, 256 devices: a whole 4x4x8 slice. The times are simulated.
256 devices in a mesh: pipe: 8 (over x_hi, y), expert: 32 (over x_lo, z, core).
Axes of the slice: x: 4 (x_hi: 2, x_lo: 2; x = x_hi * 2 + x_lo), y: 4, z: 8, core: 2. Of those that a mesh axis runs over, the one named last changes fastest.
Arguments:
- hidden_a: bfloat16 [8, 4096, 2048], P('pipe', 'expert'), may hold values from -4.5 to 4.5
- expert_ids_a: int32 [8, 4096, 8], P('pipe', 'expert'), may hold values from 0 to 127, as said below
- router_probs_a: float32 [8, 4096, 8], P('pipe', 'expert'), may hold values from 0.02 to 1
- hidden_b: bfloat16 [8, 4096, 2048], P('pipe', 'expert'), may hold values from -4.5 to 4.5
- expert_ids_b: int32 [8, 4096, 8], P('pipe', 'expert'), may hold values from 0 to 127, as said below
- router_probs_b: float32 [8, 4096, 8], P('pipe', 'expert'), may hold values from 0.02 to 1
- grad_out_b: bfloat16 [8, 4096, 2048], P('pipe', 'expert'), may hold values from -6 to 6
- norm_gain: float32 [8, 2048], P('pipe'), may hold values from 0.5 to 2
- w_gate: bfloat16 [8, 32, 2048, 768], P('pipe', 'expert'), may hold values from -0.125 to 0.125
- w_up: bfloat16 [8, 32, 2048, 768], P('pipe', 'expert'), may hold values from -0.125 to 0.125
- w_down: bfloat16 [8, 32, 768, 2048], P('pipe', 'expert'), may hold values from -0.21875 to 0.21875
Outputs:
- next_hidden_a: bfloat16 [8, 4096, 2048], P('pipe', 'expert')
- grad_in_b: bfloat16 [8, 4096, 2048], P('pipe', 'expert')
Inputs may be any that keep to these rules, and one draw needn't show every extreme that they name: `expert_ids_a`: position k of every token names an expert of k * 16 to (k + 1) * 16 - 1. In each aligned block of 128 tokens (the tokens of one device), for each position one expert (the hot one) is named by exactly 16 tokens; it is the same in all blocks and sections and in both micro-batches, and for position 0 it lies below min(16, 32). Every other expert is named by at most 8 tokens of a block, and in every block and position one of them by exactly 8. `expert_ids_b`: position k of every token names an expert of k * 16 to (k + 1) * 16 - 1. In each aligned block of 128 tokens (the tokens of one device), for each position one expert (the hot one) is named by exactly 16 tokens; it is the same in all blocks and sections and in both micro-batches, and for position 0 it lies below min(16, 32). Every other expert is named by at most 8 tokens of a block, and in every block and position one of them by exactly 8.
All inputs are finite; a program needn't handle non-finite values.
Results may differ from a plain program's by a relative error of at most 0.0066.
Values may be sent and summed in bfloat16 or wider, within the bound.
A program may use at most 128 MiB of HBM per device.

v0:
```python
import jax
import jax.numpy as jnp
from jax import lax
from jax.experimental import pallas as pl
from jax.experimental.pallas import tpu as pltpu
from jax.sharding import PartitionSpec as P

NORM_EPS = 1e-06
MESH = pl.DeviceIdType.MESH
BF = jnp.bfloat16
F32 = jnp.float32
RING = 8
ORDER = (4, 3, 5, 2, 6, 1, 7, 0)
PLACE = {k: s for s, k in enumerate(ORDER)}
GROUPS = ((0, 1), (1, 3), (3, 5), (5, 8))
TILE = 256

ARRIVALS = (
    ((4, 1), (3, 1), (5, 1), (2, 1), (6, 1), "L1", "S1", (1, 1), (7, 1)),
    ((4, 2), (3, 2), (5, 2), (2, 2), (6, 2), "L2", "S2"),
    ((4, 3), (3, 3), (5, 3), "L3", "S3"),
    ((4, 4), "L4"),
)


def hops_of(k):
    return k if k <= 4 else RING - k


HOPS = [(k, h) for k in range(1, RING) for h in range(1, hops_of(k) + 1)]
SLOT = {kh: i for i, kh in enumerate(HOPS)}


def last_dot(left, right):
    return lax.dot_general(left, right, (((1,), (1,)), ((), ())), preferred_element_type=F32)


def dot(left, right):
    return jnp.dot(left, right, preferred_element_type=F32)


def kernel(
    ids_ref, probs_a, probs_b, hid_a, hid_b, grad_b, gain_ref, wg_hbm, wu_hbm, wd_hbm,
    next_ref, prev_ref,
    wg, wu, wd, nn, gg, dd_a, dd_b, ddt_a, ddt_b, hot_a, hot_b,
    send1_a, send1_b, one_a, one_b, esend_a, esend_b,
    ring_a, ring_b, emine_a, emine_b, epart_a, epart_b,
    x_a, x_b, s_b, hid1, hid2, out_a, out_b, back_a, back_b, epin_a, epin_b,
    chain_a, chain_b, etot_a, etot_b, ein_a, ein_b, fin_a, fin_b,
    ret, dnorm, pipe_a, pipe_b, send_sems, recv_sems, local_sems,
):
    pipe = lax.axis_index("pipe")
    pipes = lax.axis_size("pipe")
    me = lax.axis_index("expert")
    core = lax.rem(me, 2)
    z = lax.rem(lax.div(me, 2), RING)
    x = lax.div(me, 2 * RING)
    sg = 1 - 2 * core
    width = hid_a.shape[1]
    half = width // 2
    ff = wg.shape[1]
    tokens = hid_a.shape[0]

    def device(xx, zz, cc):
        return {"expert": (xx * RING + zz) * 2 + cc}

    partner = [
        device(x if q < 2 else 1 - x, z, core if q % 2 == 0 else 1 - core) for q in range(4)
    ]
    long_way = device(x, lax.rem(z + sg + RING, RING), core)
    short_way = device(x, lax.rem(z - sg + RING, RING), core)
    pipe_next = {"pipe": lax.rem(pipe + 1, pipes)}
    pipe_prev = {"pipe": lax.rem(pipe + pipes - 1, pipes)}

    used = [0]
    sent = []

    def describe(src, dst, target):
        i = used[0]
        used[0] += 1
        return pltpu.make_async_remote_copy(
            src_ref=src, dst_ref=dst, send_sem=send_sems.at[i], recv_sem=recv_sems.at[i],
            device_id=target, device_id_type=MESH,
        )

    def send(src, dst, target):
        copy = describe(src, dst, target)
        copy.start()
        sent.append(copy)
        return copy

    weights = []
    for i, (src, dst) in enumerate(((wg_hbm, wg), (wu_hbm, wu), (wd_hbm, wd))):
        copy = pltpu.make_async_copy(src, dst, local_sems.at[i])
        copy.start()
        weights.append(copy)

    barrier = pltpu.get_barrier_semaphore()
    greeted = [partner[1], partner[2], partner[3], long_way, short_way]
    if pipes > 1:
        greeted += [pipe_next, pipe_prev]
    for other in greeted:
        pl.semaphore_signal(barrier, inc=1, device_id=other, device_id_type=MESH)

    def routing(which, dd, ddt, hot):
        ids = ids_ref[which]
        j = lax.broadcasted_iota(jnp.int32, (32, tokens), 0)
        q = j & 3
        s = j >> 2
        k = jnp.where((s & 1) == 1, 3 - (s >> 1), 4 + (s >> 1))
        cq = (core + (q & 1)) & 1
        xq = (x + (q >> 1)) & 1
        zq = (z + (1 - 2 * cq) * k + RING) & (RING - 1)
        expert = (xq * RING + zq) * 2 + cq
        match = (ids[0:1, :] == expert) | (ids[1:2, :] == expert)
        matched = jnp.where(match, 1.0, 0.0)
        t0 = lax.broadcasted_iota(jnp.int32, (tokens, tokens), 0)
        t1 = lax.broadcasted_iota(jnp.int32, (tokens, tokens), 1)
        rank = dot(matched.astype(BF), jnp.where(t0 < t1, 1.0, 0.0).astype(BF))
        ranked = jnp.where(match, rank, 200.0)
        own = q < 2
        rank_own = jnp.sum(jnp.where(own, matched * rank, 0.0), axis=0, keepdims=True)
        rank_other = jnp.sum(jnp.where(own, 0.0, matched * rank), axis=0, keepdims=True)
        hot[...] = dot(matched.astype(BF), jnp.ones((tokens, TILE), BF))
        r = lax.broadcasted_iota(jnp.int32, (256, 32), 0)
        cols = lax.broadcasted_iota(jnp.int32, (256, 32), 1)
        spread = jnp.where((r >> 3) == cols, 1.0, 0.0).astype(BF)
        rows = dot(spread, ranked.astype(BF))
        r = lax.broadcasted_iota(jnp.int32, (256, tokens), 0)
        hit = rows == (r & 7).astype(F32)
        mine = ((r >> 3) & 3) < 2
        dd[0:256, 0:tokens] = jnp.where(hit & mine, 1.0, 0.0).astype(BF)
        dd[0:256, tokens:] = jnp.where(hit & jnp.logical_not(mine), 1.0, 0.0).astype(BF)
        r = lax.broadcasted_iota(jnp.int32, (128, tokens), 0)
        rf = r.astype(F32)
        dd[256:384, 0:tokens] = jnp.where((rank_own == rf + 8.0) & (r < 8), 1.0, 0.0).astype(BF)
        dd[256:384, tokens:] = jnp.where(
            (rank_other == rf) & (r >= 8) & (r < 16), 1.0, 0.0
        ).astype(BF)
        t0 = lax.broadcasted_iota(jnp.int32, (2 * tokens, 2 * tokens), 0)
        t1 = lax.broadcasted_iota(jnp.int32, (2 * tokens, 2 * tokens), 1)
        eye = jnp.where(t0 == t1, 1.0, 0.0).astype(BF)
        ddt[...] = last_dot(eye, dd[...]).astype(BF)

    xf = x.astype(F32)

    def gates(probs):
        weight = probs / jnp.sum(probs, axis=-1, keepdims=True)
        first, second = weight[:, 0:1], weight[:, 1:2]
        return first * (1.0 - xf) + second * xf, second * (1.0 - xf) + first * xf

    def inverse_norm(values):
        return lax.rsqrt(jnp.mean(values * values, axis=-1, keepdims=True) + NORM_EPS)

    def prepare(hidden, probs, gradient):
        @pl.loop(0, tokens // 16)
        def _(i):
            rows = pl.ds(pl.multiple_of(i * 16, 16), 16)
            later = pl.ds(pl.multiple_of(tokens + i * 16, 16), 16)
            values = hidden[rows, :].astype(F32)
            normed = (values * inverse_norm(values) * gain_ref[...]).astype(BF)
            nn[rows, :] = normed
            nn[later, :] = normed
            if gradient is not None:
                own, other = gates(probs[rows, :])
                up = gradient[rows, :].astype(F32)
                gg[rows, :] = (own * up).astype(BF)
                gg[later, :] = (other * up).astype(BF)

    def pack(dd, send1, one, emine, esend, first, second, wide):
        step = min(512, wide)

        @pl.loop(0, wide // step)
        def _(i):
            cols = pl.ds(pl.multiple_of(i * step, step), step)
            top = dot(dd[0:272, :], first(i * step, step))
            low = dot(dd[0:272, :], second(i * step, step))
            both = jnp.concatenate(
                [top.reshape(34, 8, step), low.reshape(34, 8, step)], axis=1
            ).astype(BF)
            blocks = both[0:32].reshape(8, 4, 16, step)
            one[:, 0, :, cols] = blocks[:, 0]
            send1[:, :, :, cols] = blocks[:, 1:4]
            emine[0, 0, :, cols] = both[32]
            esend[:, cols] = both[33]

    def columns(ref, base):
        def take(start, size):
            return ref[:, pl.ds(pl.multiple_of(base + start, size), size)]

        return take

    class Dispatch:
        def __init__(self, send1, one, esend, emine, epart, ring, unpack):
            self.send1, self.one, self.esend, self.emine = send1, one, esend, emine
            self.epart, self.ring, self.unpack = epart, ring, unpack
            self.hop = {}
            self.part = {}

        def exchange(self):
            self.first = []
            self.e_first = None
            for n, (a, b) in enumerate(GROUPS):
                at = pl.ds(a, b - a)
                self.first.append([
                    send(self.send1.at[at, q - 1], self.one.at[at, q], partner[q])
                    for q in (1, 2, 3)
                ])
                if n == 2:
                    self.e_first = send(self.esend, self.emine.at[0, 1], partner[2])

        def forward(self, k, h):
            src = self.one.at[PLACE[k]] if h == 1 else self.ring.at[SLOT[k, h - 1]]
            target = long_way if k <= 4 else short_way
            self.hop[k, h] = send(src, self.ring.at[SLOT[k, h]], target)

        def forward_extra(self, way, h):
            if way == "L":
                copy = send(self.emine.at[h - 1], self.emine.at[h], long_way)
            else:
                copy = send(self.emine.at[(9 - h) % 8], self.emine.at[8 - h], short_way)
            self.hop[way, h] = copy

        def swap_extra(self, k):
            self.part[k] = send(self.emine.at[k], self.epart.at[k], partner[1])

        def launch(self, group):
            for copy in self.first[group]:
                copy.wait_recv()
            for s in range(*GROUPS[group]):
                if ORDER[s]:
                    self.forward(ORDER[s], 1)
            if group == 2:
                self.e_first.wait_recv()
                self.forward_extra("L", 1)
                self.forward_extra("S", 1)
                self.swap_extra(0)

        def local(self):
            self.unpack(self.one.at[PLACE[0]], 0)
            self.unpack(self.emine.at[0], 256)

        def arrive(self, event):
            if isinstance(event, str):
                way, h = event[0], int(event[1])
                self.hop[way, h].wait_recv()
                if h < (4 if way == "L" else 3):
                    self.forward_extra(way, h + 1)
                k = h if way == "L" else 8 - h
                self.swap_extra(k)
                self.unpack(self.emine.at[k], 256 + k * 16)
            else:
                k, h = event
                self.hop[k, h].wait_recv()
                if h < hops_of(k):
                    self.forward(k, h + 1)
                else:
                    self.unpack(self.ring.at[SLOT[k, h]], k * 32)

        def finish(self):
            for k in (0, 1, 7, 2, 6, 3, 5, 4):
                self.part[k].wait_recv()
                self.unpack(self.epart.at[k], 384 + k * 16)

    def unpack_b(src, row):
        count = src.shape[0]
        values = src[...].astype(F32).reshape(count, 2, 8, width)
        rows = pl.ds(row, count * 8)
        x_b[rows, :] = values[:, 0].reshape(count * 8, width).astype(BF)
        s_b[rows, :] = values[:, 1].reshape(count * 8, width).astype(BF)

    def unpack_a(src, row):
        count = src.shape[0]
        values = src[...].astype(F32).reshape(count, 2, 8, half)
        rows = pl.ds(row, count * 8)
        x_a[rows, 0:half] = values[:, 0].reshape(count * 8, half).astype(BF)
        x_a[rows, half:] = values[:, 1].reshape(count * 8, half).astype(BF)

    def tile_at(i):
        return pl.ds(pl.multiple_of(i * TILE, TILE), TILE)

    def forward_units(i):
        cols = tile_at(i)
        gate_pre = dot(x_a[...], wg[:, cols])
        up_pre = dot(x_a[...], wu[:, cols])
        hid1[:, cols] = (gate_pre * jax.nn.sigmoid(gate_pre) * up_pre).astype(BF)

    def backward_units(i):
        cols = tile_at(i)
        gate_pre = dot(x_b[...], wg[:, cols])
        up_pre = dot(x_b[...], wu[:, cols])
        d_hidden = last_dot(s_b[...], wd[cols, :])
        sigma = jax.nn.sigmoid(gate_pre)
        hid1[:, cols] = (d_hidden * up_pre * sigma * (1.0 + gate_pre * (1.0 - sigma))).astype(BF)
        hid2[:, cols] = (d_hidden * gate_pre * sigma).astype(BF)

    def store_out(out, hot, i, low, high):
        valid = jnp.broadcast_to(hot[28:29, :], (256, TILE)) > 8.5
        both = []
        for part in (low, high):
            extra = jnp.where(valid, part[256:512], 0.0)
            both.append(jnp.concatenate([part[0:256], extra], axis=0).reshape(64, 8, TILE))
        out[:, :, tile_at(i)] = jnp.concatenate(both, axis=1).astype(BF)

    def forward_out(i):
        low = dot(hid1[...], wd[:, tile_at(i)])
        high = dot(hid1[...], wd[:, pl.ds(pl.multiple_of(half + i * TILE, TILE), TILE)])
        store_out(out_a, hot_a, i, low, high)

    def backward_out(i):
        later = pl.ds(pl.multiple_of(half + i * TILE, TILE), TILE)
        low = last_dot(hid1[...], wg[tile_at(i), :]) + last_dot(hid2[...], wu[tile_at(i), :])
        high = last_dot(hid1[...], wg[later, :]) + last_dot(hid2[...], wu[later, :])
        store_out(out_b, hot_b, i, low, high)

    def run(step, first, last):
        @pl.loop(first, last)
        def _(i):
            step(i)

    class Return:
        def __init__(self, out, back, epin, chain, etot, ein, fin):
            self.out, self.back, self.epin, self.chain = out, back, epin, chain
            self.etot, self.ein, self.fin = etot, ein, fin
            self.hop = {}
            self.last = []

        def swap(self):
            self.swapped = send(self.out.at[pl.ds(48, 16)], self.epin, partner[1])

        def forward(self, k, h):
            src = self.out.at[pl.ds(4 * k, 4)] if h == 1 else self.back.at[SLOT[k, h - 1]]
            target = short_way if k <= 4 else long_way
            self.hop[k, h] = send(src, self.back.at[SLOT[k, h]], target)

        def launch(self):
            self.swap()
            for s in range(7):
                self.forward(ORDER[s], 1)

        def launch_extra(self):
            self.swapped.wait_recv()
            self.epin[...] = (self.out[32:48].astype(F32) + self.epin[...].astype(F32)).astype(BF)
            self.hop["L", 1] = send(self.epin.at[pl.ds(8, 2)], self.chain.at[0], short_way)
            self.hop["S", 1] = send(self.epin.at[pl.ds(10, 2)], self.chain.at[4], long_way)

        def distribute(self, k):
            src = self.out.at[pl.ds(0, 4)] if k == 0 else self.back.at[SLOT[k, hops_of(k)]]
            for q in (2, 3, 1):
                self.last.append(send(src.at[q], self.fin.at[k, q - 1], partner[q]))

        def arrive(self, event):
            if isinstance(event, str):
                way, h = event[0], int(event[1])
                self.hop[way, h].wait_recv()
                k = 4 - h if way == "L" else 5 + h
                at = h - 1 if way == "L" else 3 + h
                if h < (4 if way == "L" else 3):
                    mine = self.epin[2 * k:2 * k + 2].astype(F32)
                    self.chain[at] = (self.chain[at].astype(F32) + mine).astype(BF)
                    target = short_way if way == "L" else long_way
                    self.hop[way, h + 1] = send(
                        self.chain.at[at], self.chain.at[at + 1], target
                    )
            else:
                k, h = event
                self.hop[k, h].wait_recv()
                if h < hops_of(k):
                    self.forward(k, h + 1)
                else:
                    self.distribute(k)

        def finish_extra(self):
            total = self.epin[0:2].astype(F32) + self.chain[3].astype(F32)
            self.etot[...] = (total + self.chain[6].astype(F32)).astype(BF)
            self.last.append(send(self.etot.at[1], self.ein, partner[2]))

        def collect(self):
            for copy in self.last:
                copy.wait_recv()
            for k in range(RING):
                own = self.out[0:1] if k == 0 else self.back[SLOT[k, hops_of(k)], 0:1]
                block = jnp.concatenate([own.astype(F32), self.fin[k].astype(F32)], axis=0)
                block = block.reshape(4, 2, 8, half)
                at = PLACE[k] * 32
                ret[at:at + 32, 0:half] = block[:, 0].reshape(32, half).astype(BF)
                ret[at:at + 32, half:] = block[:, 1].reshape(32, half).astype(BF)
            own, other = self.etot[0].astype(F32), self.ein[...].astype(F32)
            ret[256:272, 0:half] = jnp.concatenate([own[0:8], other[0:8]], axis=0).astype(BF)
            ret[256:272, half:] = jnp.concatenate([own[8:16], other[8:16]], axis=0).astype(BF)

    dis_a = Dispatch(send1_a, one_a, esend_a, emine_a, epart_a, ring_a, unpack_a)
    dis_b = Dispatch(send1_b, one_b, esend_b, emine_b, epart_b, ring_b, unpack_b)
    ret_a = Return(out_a, back_a, epin_a, chain_a, etot_a, ein_a, fin_a)
    ret_b = Return(out_b, back_b, epin_b, chain_b, etot_b, ein_b, fin_b)

    routing(1, dd_b, ddt_b, hot_b)
    prepare(hid_b, probs_b, grad_b)
    pack(dd_b, send1_b, one_b, emine_b, esend_b, columns(nn, 0), columns(gg, 0), width)
    pl.semaphore_wait(barrier, len(greeted))
    dis_b.exchange()

    routing(0, dd_a, ddt_a, hot_a)
    prepare(hid_a, probs_a, None)
    pack(dd_a, send1_a, one_a, emine_a, esend_a, columns(nn, 0), columns(nn, half), half)
    ret[272:384, :] = jnp.zeros((112, width), BF)

    for group in range(4):
        dis_b.launch(group)
    dis_a.exchange()
    dis_b.local()
    for event in ARRIVALS[0] + ARRIVALS[1]:
        dis_b.arrive(event)
    for group in range(4):
        dis_a.launch(group)
    dis_a.local()
    for event in ARRIVALS[2] + ARRIVALS[3]:
        dis_b.arrive(event)
    dis_b.finish()
    for copy in weights:
        copy.wait()

    tiles = ff // TILE
    for event in ARRIVALS[0]:
        dis_a.arrive(event)
    run(backward_units, 0, tiles)
    for event in ARRIVALS[1]:
        dis_a.arrive(event)
    outs = half // TILE
    run(backward_out, 0, outs)
    ret_b.launch()
    for event in ARRIVALS[2] + ARRIVALS[3]:
        dis_a.arrive(event)
    ret_b.launch_extra()
    ret_b.distribute(0)
    dis_a.finish()
    for event in ARRIVALS[0]:
        ret_b.arrive(event)
    run(forward_units, 0, tiles)
    for event in ARRIVALS[1]:
        ret_b.arrive(event)
    run(forward_out, 0, outs)
    ret_a.launch()
    for event in ARRIVALS[2] + ARRIVALS[3]:
        ret_b.arrive(event)
    ret_b.finish_extra()
    ret_a.launch_extra()
    ret_a.distribute(0)
    for event in ARRIVALS[0]:
        ret_a.arrive(event)
    ret_b.collect()

    step = min(512, width)

    @pl.loop(0, width // step)
    def _(i):
        cols = pl.ds(pl.multiple_of(i * step, step), step)
        moved = dot(ddt_b[...], ret[:, cols])
        dnorm[:, cols] = moved[0:tokens] + moved[tokens:]

    @pl.loop(0, tokens // 16)
    def _(i):
        rows = pl.ds(pl.multiple_of(i * 16, 16), 16)
        values = hid_b[rows, :].astype(F32)
        r = inverse_norm(values)
        scaled = dnorm[rows, :] * gain_ref[...]
        inner = jnp.mean(values * scaled, axis=-1, keepdims=True)
        grown = grad_b[rows, :].astype(F32) + r * scaled - values * (r * r * r * inner)
        pipe_b[rows, :] = grown.astype(BF)

    to_prev = describe(pipe_b, prev_ref, pipe_prev)
    if pipes > 1:
        @pl.when(pipe > 0)
        def _():
            to_prev.start()

    for event in ARRIVALS[1] + ARRIVALS[2] + ARRIVALS[3]:
        ret_a.arrive(event)
    ret_a.finish_extra()
    ret_a.collect()

    own_gate, other_gate = gates(probs_a[...])

    @pl.loop(0, width // step)
    def _(i):
        cols = pl.ds(pl.multiple_of(i * step, step), step)
        moved = dot(ddt_a[...], ret[:, cols])
        summed = own_gate * moved[0:tokens] + other_gate * moved[tokens:]
        pipe_a[:, cols] = (hid_a[:, cols].astype(F32) + summed).astype(BF)

    to_next = describe(pipe_a, next_ref, pipe_next)
    if pipes > 1:
        @pl.when(pipe < pipes - 1)
        def _():
            to_next.start()

    @pl.when(pipe == 0)
    def _():
        next_ref[...] = jnp.zeros(next_ref.shape, BF)

    @pl.when(pipe == pipes - 1)
    def _():
        prev_ref[...] = jnp.zeros(prev_ref.shape, BF)

    for copy in sent:
        copy.wait_send()
    if pipes > 1:
        @pl.when(pipe < pipes - 1)
        def _():
            to_prev.wait_recv()
            to_next.wait_send()

        @pl.when(pipe > 0)
        def _():
            to_next.wait_recv()
            to_prev.wait_send()


def scratch(tokens, width, ff):
    half = width // 2
    vmem = pltpu.VMEM
    hops = len(HOPS)
    shapes = [
        ((width, ff), BF), ((width, ff), BF), ((ff, width), BF),
        ((2 * tokens, width), BF), ((2 * tokens, width), BF),
        ((384, 2 * tokens), BF), ((384, 2 * tokens), BF),
        ((2 * tokens, 384), BF), ((2 * tokens, 384), BF),
        ((32, TILE), F32), ((32, TILE), F32),
        ((8, 3, 16, half), BF), ((8, 3, 16, width), BF),
        ((8, 4, 16, half), BF), ((8, 4, 16, width), BF),
        ((16, half), BF), ((16, width), BF),
        ((hops, 4, 16, half), BF), ((hops, 4, 16, width), BF),
        ((8, 2, 16, half), BF), ((8, 2, 16, width), BF),
        ((8, 2, 16, half), BF), ((8, 2, 16, width), BF),
        ((512, width), BF), ((512, width), BF), ((512, width), BF),
        ((512, ff), BF), ((512, ff), BF),
        ((64, 16, half), BF), ((64, 16, half), BF),
        ((hops, 4, 16, half), BF), ((hops, 4, 16, half), BF),
        ((16, 16, half), BF), ((16, 16, half), BF),
        ((7, 2, 16, half), BF), ((7, 2, 16, half), BF),
        ((2, 16, half), BF), ((2, 16, half), BF),
        ((16, half), BF), ((16, half), BF),
        ((8, 3, 16, half), BF), ((8, 3, 16, half), BF),
        ((384, width), BF), ((tokens, width), F32),
        ((tokens, width), BF), ((tokens, width), BF),
    ]
    messages = 256
    return [vmem(shape, kind) for shape, kind in shapes] + [
        pltpu.SemaphoreType.DMA((messages,)),
        pltpu.SemaphoreType.DMA((messages,)),
        pltpu.SemaphoreType.DMA((3,)),
    ]


def per_device(
    hidden_a, expert_ids_a, router_probs_a, hidden_b, expert_ids_b, router_probs_b,
    grad_out_b, norm_gain, w_gate, w_up, w_down,
):
    tokens, width = hidden_a.shape[1:]
    ff = w_gate.shape[3]
    ids = jnp.swapaxes(jnp.concatenate([expert_ids_a, expert_ids_b], axis=0), 1, 2)
    inside = pl.BlockSpec(memory_space=pltpu.VMEM)
    outside = pl.BlockSpec(memory_space=pl.ANY)
    result = jax.ShapeDtypeStruct((tokens, width), BF)
    rows = 512
    next_hidden, grad_before = pl.pallas_call(
        kernel,
        out_shape=(result, result),
        in_specs=[inside] * 7 + [outside] * 3,
        out_specs=(inside, inside),
        scratch_shapes=scratch(tokens, width, ff),
        compiler_params=pltpu.CompilerParams(
            collective_id=0, has_side_effects=True, vmem_limit_bytes=60 * 1024 * 1024
        ),
        cost_estimate=pl.CostEstimate(
            flops=2 * rows * width * ff * 8, bytes_accessed=6 * width * ff, transcendentals=0
        ),
    )(
        ids, router_probs_a[0], router_probs_b[0], hidden_a[0], hidden_b[0], grad_out_b[0],
        norm_gain, w_gate[0, 0], w_up[0, 0], w_down[0, 0],
    )
    return next_hidden[None], grad_before[None]


def solution(mesh):
    in_specs = (
        P("pipe", "expert", None),
        P("pipe", "expert", None),
        P("pipe", "expert", None),
        P("pipe", "expert", None),
        P("pipe", "expert", None),
        P("pipe", "expert", None),
        P("pipe", "expert", None),
        P("pipe", None),
        P("pipe", "expert", None, None),
        P("pipe", "expert", None, None),
        P("pipe", "expert", None, None),
    )
    out_specs = (P("pipe", "expert", None), P("pipe", "expert", None))
    return jax.shard_map(
        per_device, mesh=mesh, in_specs=in_specs, out_specs=out_specs, check_vma=False
    )
```

profile of v0, /device:TPU:6, one launch (start us, length us, event | category | flops | bytes accessed | tf_op | source)
XLA Modules:
  0.0 201.9 jit_solution(17434049231967689191)
XLA Ops:
  0.6 1.3 add_bitcast_fusion.ids_ref
  1.9 1.4 copy.13
  3.3 1.4 copy.14
  4.8 193.4 %shard_map.122 = (bf16[128,2048]{1,0:T(8,128)(2,1)}, bf16[128,2048]{1,0:T(8,128)(2,1)}) custom-call(s32[2,8,128]{2,1,0:T(8,128)} %add_bitcast_fusion.ids_ref, f32[128,8]{1,0:T(8,128)} %bitcast.14, f32[128,8]{1,0:T(8,128)} %bitcast.15, bf16[128,2048]{1,0:T(8,128)(2,1)} %bitcast.19, bf16[128,2048]{1,0:T(8,128)(2,1)} %bitcast.20, bf16[128,2048]{1,0:T(8,128)(2,1)} %bitcast.21, ...), custom_call_target="tpu_custom_call" | custom-call | flops 12884901888 | bytes 9437184 | tf_op jit(solution)/shard_map/pallas_call | solution.py:566
  198.2 1.9 copy.17
  200.1 1.9 copy.18
where the time goes:
time: 203 us; the launch traced here: 202 us
  Pallas kernels  193 us (95%)
  local copies, waits for them, and re-layouts  6.59 us (3%)
    pallas_call x1, Pallas kernels, per_device(): pl.pallas_call(kernel, out_shape=(result, result), in_specs=[inside] * 7...  193 us
    unnamed x4, local copies, waits for them, and re-layouts  6.59 us

commit v1 on v0

v1 whole, which is shorter than its diff:
```python
import jax
import jax.numpy as jnp
from jax import lax
from jax.experimental import pallas as pl
from jax.experimental.pallas import tpu as pltpu
from jax.sharding import PartitionSpec as P

NORM_EPS = 1e-06
MESH = pl.DeviceIdType.MESH
BF = jnp.bfloat16
F32 = jnp.float32
RING = 8
ORDER = (4, 3, 5, 2, 6, 1, 7, 0)
PLACE = {k: s for s, k in enumerate(ORDER)}
TILE = 256
PARTS_A = 2
BLOCKS = [(k, q) for k in ORDER for q in (2, 3, 0, 1) if (k, q) != (0, 0)]
EXTRA_HOPS = {"L": 4, "S": 3}


def chunks(count):
    size = -(-len(BLOCKS) // count)
    return [BLOCKS[i:i + size] for i in range(0, len(BLOCKS), size)]


def last_dot(left, right):
    return lax.dot_general(left, right, (((1,), (1,)), ((), ())), preferred_element_type=F32)


def dot(left, right):
    return jnp.dot(left, right, preferred_element_type=F32)


def kernel(
    ids_ref, probs_ref, hid_a, hid_b, grad_b, gain_ref, wg_hbm, wu_hbm, wd_hbm,
    next_ref, prev_ref,
    wg, wu, wd, nn, gg, dd_a, dd_b, ddt_a, ddt_b, hot_a, hot_b, gates_a, gates_b,
    send1_a, send1_b, rx_a, rx_b, esend_a, esend_b, emine_a, emine_b, epart_a, epart_b,
    x_a, x_b, s_b, hid1, hid2, out_a, out_b, epin_a, epin_b,
    chain_a, chain_b, etot_a, etot_b, ein_a, ein_b, fin_a, fin_b,
    ret, dnorm, pipe_a, pipe_b, send_sems, recv_sems, local_sems,
):
    pipe = lax.axis_index("pipe")
    pipes = lax.axis_size("pipe")
    me = lax.axis_index("expert")
    core = lax.rem(me, 2)
    z = lax.rem(lax.div(me, 2), RING)
    x = lax.div(me, 2 * RING)
    sg = 1 - 2 * core
    width = hid_a.shape[1]
    half = width // 2
    ff = wg.shape[1]
    tokens = hid_a.shape[0]

    def device(xx, zz, cc):
        return {"expert": (xx * RING + zz) * 2 + cc}

    partner = [
        device(x if q < 2 else 1 - x, z, core if q % 2 == 0 else 1 - core) for q in range(4)
    ]

    def target(k, q):
        cc = core if q % 2 == 0 else 1 - core
        return device(x if q < 2 else 1 - x, lax.rem(z + (1 - 2 * cc) * k + RING, RING), cc)

    def source(k, q):
        cc = core if q % 2 == 0 else 1 - core
        return device(x if q < 2 else 1 - x, lax.rem(z - sg * k + RING, RING), cc)

    long_way = device(x, lax.rem(z + sg + RING, RING), core)
    short_way = device(x, lax.rem(z - sg + RING, RING), core)
    pipe_next = {"pipe": lax.rem(pipe + 1, pipes)}
    pipe_prev = {"pipe": lax.rem(pipe + pipes - 1, pipes)}

    used = [0]
    sent = []

    def describe(src, dst, target):
        i = used[0]
        used[0] += 1
        return pltpu.make_async_remote_copy(
            src_ref=src, dst_ref=dst, send_sem=send_sems.at[i], recv_sem=recv_sems.at[i],
            device_id=target, device_id_type=MESH,
        )

    def send(src, dst, target):
        copy = describe(src, dst, target)
        copy.start()
        sent.append(copy)
        return copy

    weights = []
    for i, (src, dst) in enumerate(((wg_hbm, wg), (wu_hbm, wu), (wd_hbm, wd))):
        copy = pltpu.make_async_copy(src, dst, local_sems.at[i])
        copy.start()
        weights.append(copy)

    barrier = pltpu.get_barrier_semaphore()
    greeted = [target(k, q) for k, q in BLOCKS]
    if pipes > 1:
        greeted += [pipe_next, pipe_prev]
    for other in greeted:
        pl.semaphore_signal(barrier, inc=1, device_id=other, device_id_type=MESH)

    def routing(which, dd, ddt, hot):
        ids = ids_ref[which]
        j = lax.broadcasted_iota(jnp.int32, (32, tokens), 0)
        q = j & 3
        s = j >> 2
        k = jnp.where((s & 1) == 1, 3 - (s >> 1), 4 + (s >> 1))
        cq = (core + (q & 1)) & 1
        xq = (x + (q >> 1)) & 1
        zq = (z + (1 - 2 * cq) * k + RING) & (RING - 1)
        expert = (xq * RING + zq) * 2 + cq
        match = (ids[0:1, :] == expert) | (ids[1:2, :] == expert)
        matched = jnp.where(match, 1.0, 0.0)
        t0 = lax.broadcasted_iota(jnp.int32, (tokens, tokens), 0)
        t1 = lax.broadcasted_iota(jnp.int32, (tokens, tokens), 1)
        rank = dot(matched.astype(BF), jnp.where(t0 < t1, 1.0, 0.0).astype(BF))
        ranked = jnp.where(match, rank, 200.0)
        own = q < 2
        rank_own = jnp.sum(jnp.where(own, matched * rank, 0.0), axis=0, keepdims=True)
        rank_other = jnp.sum(jnp.where(own, 0.0, matched * rank), axis=0, keepdims=True)
        hot[...] = dot(matched.astype(BF), jnp.ones((tokens, TILE), BF))
        r = lax.broadcasted_iota(jnp.int32, (256, 32), 0)
        cols = lax.broadcasted_iota(jnp.int32, (256, 32), 1)
        spread = jnp.where((r >> 3) == cols, 1.0, 0.0).astype(BF)
        rows = dot(spread, ranked.astype(BF))
        r = lax.broadcasted_iota(jnp.int32, (256, tokens), 0)
        hit = rows == (r & 7).astype(F32)
        mine = ((r >> 3) & 3) < 2
        dd[0:256, 0:tokens] = jnp.where(hit & mine, 1.0, 0.0).astype(BF)
        dd[0:256, tokens:] = jnp.where(hit & jnp.logical_not(mine), 1.0, 0.0).astype(BF)
        r = lax.broadcasted_iota(jnp.int32, (128, tokens), 0)
        rf = r.astype(F32)
        dd[256:384, 0:tokens] = jnp.where((rank_own == rf + 8.0) & (r < 8), 1.0, 0.0).astype(BF)
        dd[256:384, tokens:] = jnp.where(
            (rank_other == rf) & (r >= 8) & (r < 16), 1.0, 0.0
        ).astype(BF)
        t0 = lax.broadcasted_iota(jnp.int32, (2 * tokens, 2 * tokens), 0)
        t1 = lax.broadcasted_iota(jnp.int32, (2 * tokens, 2 * tokens), 1)
        eye = jnp.where(t0 == t1, 1.0, 0.0).astype(BF)
        ddt[...] = last_dot(eye, dd[...]).astype(BF)

    xf = x.astype(F32)

    def gates(which, gate):
        probs = probs_ref[which]
        weight = probs / jnp.sum(probs, axis=0, keepdims=True)
        first, second = weight[0:1, :], weight[1:2, :]
        for i, row in enumerate(
            (first * (1.0 - xf) + second * xf, second * (1.0 - xf) + first * xf)
        ):
            gate[i] = jnp.broadcast_to(row, (tokens, tokens)).T

    def inverse_norm(values):
        return lax.rsqrt(jnp.mean(values * values, axis=-1, keepdims=True) + NORM_EPS)

    def prepare(hidden, gate, gradient):
        @pl.loop(0, tokens // 16)
        def _(i):
            rows = pl.ds(pl.multiple_of(i * 16, 16), 16)
            later = pl.ds(pl.multiple_of(tokens + i * 16, 16), 16)
            values = hidden[rows, :].astype(F32)
            normed = (values * inverse_norm(values) * gain_ref[...]).astype(BF)
            nn[rows, :] = normed
            nn[later, :] = normed
            if gradient is not None:
                up = gradient[rows, :].astype(F32)
                gg[rows, :] = (gate[0, rows, 0:1] * up).astype(BF)
                gg[later, :] = (gate[1, rows, 0:1] * up).astype(BF)

    def pack(dd, send1, rx, emine, esend, first, second, wide):
        step = min(512, wide)

        @pl.loop(0, wide // step)
        def _(i):
            cols = pl.ds(pl.multiple_of(i * step, step), step)
            top = dot(dd[0:272, :], first(i * step, step))
            low = dot(dd[0:272, :], second(i * step, step))
            both = jnp.concatenate(
                [top.reshape(34, 8, step), low.reshape(34, 8, step)], axis=1
            ).astype(BF)
            send1[:, :, :, cols] = both[0:32].reshape(8, 4, 16, step)
            rx[0, 0, :, cols] = both[4 * PLACE[0]]
            emine[0, 0, :, cols] = both[32]
            esend[:, cols] = both[33]

    def columns(ref, base):
        def take(start, size):
            return ref[:, pl.ds(pl.multiple_of(base + start, size), size)]

        return take

    class Dispatch:
        def __init__(self, send1, rx, esend, emine, epart, unpack):
            self.send1, self.rx, self.esend, self.emine = send1, rx, esend, emine
            self.epart, self.unpack = epart, unpack
            self.main, self.hop, self.part = {}, {}, {}

        def launch(self, blocks):
            for k, q in blocks:
                self.main[k, q] = send(
                    self.send1.at[PLACE[k], q], self.rx.at[k, q], target(k, q)
                )

        def start_extra(self):
            self.e_first = send(self.esend, self.emine.at[0, 1], partner[2])

        def swap_extra(self, k):
            self.part[k] = send(self.emine.at[k], self.epart.at[k], partner[1])

        def extra(self, h):
            if h == 1:
                self.e_first.wait_recv()
            for way, last in EXTRA_HOPS.items():
                if 1 < h <= last + 1:
                    self.hop[way, h - 1].wait_recv()
                if h <= last:
                    a, b = (h - 1, h) if way == "L" else ((9 - h) % RING, RING - h)
                    self.hop[way, h] = send(
                        self.emine.at[a], self.emine.at[b],
                        long_way if way == "L" else short_way,
                    )
            if h <= 5:
                for k in {h - 1, (9 - h) % RING} if h <= 4 else {4}:
                    self.swap_extra(k)

        def collect(self):
            for k in ORDER:
                for q in range(4):
                    if (k, q) != (0, 0):
                        self.main[k, q].wait_recv()
                self.unpack(self.rx.at[k], k * 32)
            for k in (0, 1, 7, 2, 6, 3, 5, 4):
                self.unpack(self.emine.at[k], 256 + k * 16)
                self.part[k].wait_recv()
                self.unpack(self.epart.at[k], 384 + k * 16)

    def unpack_b(src, row):
        count = src.shape[0]
        values = src[...].astype(F32).reshape(count, 2, 8, width)
        rows = pl.ds(row, count * 8)
        x_b[rows, :] = values[:, 0].reshape(count * 8, width).astype(BF)
        s_b[rows, :] = values[:, 1].reshape(count * 8, width).astype(BF)

    def unpack_a(src, row):
        count = src.shape[0]
        values = src[...].astype(F32).reshape(count, 2, 8, half)
        rows = pl.ds(row, count * 8)
        x_a[rows, 0:half] = values[:, 0].reshape(count * 8, half).astype(BF)
        x_a[rows, half:] = values[:, 1].reshape(count * 8, half).astype(BF)

    def tile_at(i):
        return pl.ds(pl.multiple_of(i * TILE, TILE), TILE)

    def forward_units(i):
        cols = tile_at(i)
        gate_pre = dot(x_a[...], wg[:, cols])
        up_pre = dot(x_a[...], wu[:, cols])
        hid1[:, cols] = (gate_pre * jax.nn.sigmoid(gate_pre) * up_pre).astype(BF)

    def backward_units(i):
        cols = tile_at(i)
        gate_pre = dot(x_b[...], wg[:, cols])
        up_pre = dot(x_b[...], wu[:, cols])
        d_hidden = last_dot(s_b[...], wd[cols, :])
        sigma = jax.nn.sigmoid(gate_pre)
        hid1[:, cols] = (d_hidden * up_pre * sigma * (1.0 + gate_pre * (1.0 - sigma))).astype(BF)
        hid2[:, cols] = (d_hidden * gate_pre * sigma).astype(BF)

    def store_out(out, part, hot, i, low, high):
        valid = jnp.broadcast_to(hot[28:29, :], (256, TILE)) > 8.5
        both = []
        for half_rows in (low, high):
            extra = jnp.where(valid, half_rows[256:512], 0.0)
            both.append(
                jnp.concatenate([half_rows[0:256], extra], axis=0).reshape(64, 8, TILE)
            )
        out[part, :, :, tile_at(i)] = jnp.concatenate(both, axis=1).astype(BF)

    def shifted(base, i):
        return pl.ds(pl.multiple_of(base + i * TILE, TILE), TILE)

    def forward_out(part):
        wide = out_a.shape[3]

        def step(i):
            low = dot(hid1[...], wd[:, shifted(2 * part * wide, i)])
            high = dot(hid1[...], wd[:, shifted((2 * part + 1) * wide, i)])
            store_out(out_a, part, hot_a, i, low, high)

        return step

    def backward_out(i):
        now, later = shifted(0, i), shifted(half, i)
        low = last_dot(hid1[...], wg[now, :]) + last_dot(hid2[...], wu[now, :])
        high = last_dot(hid1[...], wg[later, :]) + last_dot(hid2[...], wu[later, :])
        store_out(out_b, 0, hot_b, i, low, high)

    def run(step, first, last):
        @pl.loop(first, last)
        def _(i):
            step(i)

    class Return:
        def __init__(self, out, epin, chain, etot, ein, fin):
            self.out, self.epin, self.chain = out, epin, chain
            self.etot, self.ein, self.fin = etot, ein, fin
            self.main, self.hop = {}, {}

        def launch(self, part, blocks):
            for k, q in blocks:
                self.main[part, k, q] = send(
                    self.out.at[part, 4 * k + q], self.fin.at[part, k, q], source(k, q)
                )

        def swap(self):
            self.swapped = send(self.out.at[:, pl.ds(48, 16)], self.epin, partner[1])

        def extra(self, h):
            if h == 1:
                self.swapped.wait_recv()
                mine = self.out[:, 32:48].astype(F32)
                self.epin[...] = (mine + self.epin[...].astype(F32)).astype(BF)
                self.hop["L", 1] = send(
                    self.epin.at[:, pl.ds(8, 2)], self.chain.at[0], short_way
                )
                self.hop["S", 1] = send(
                    self.epin.at[:, pl.ds(10, 2)], self.chain.at[4], long_way
                )
                return
            for way, last in EXTRA_HOPS.items():
                if h > last:
                    continue
                self.hop[way, h - 1].wait_recv()
                k, at = (5 - h, h - 2) if way == "L" else (4 + h, 2 + h)
                mine = self.epin[:, 2 * k:2 * k + 2].astype(F32)
                self.chain[at] = (self.chain[at].astype(F32) + mine).astype(BF)
                self.hop[way, h] = send(
                    self.chain.at[at], self.chain.at[at + 1],
                    short_way if way == "L" else long_way,
                )

        def finish_extra(self):
            self.hop["L", 4].wait_recv()
            self.hop["S", 3].wait_recv()
            total = self.epin[:, 0:2].astype(F32) + self.chain[3].astype(F32)
            self.etot[...] = (total + self.chain[6].astype(F32)).astype(BF)
            self.e_last = send(self.etot.at[:, 1], self.ein, partner[2])

        def collect(self, part):
            wide = self.out.shape[3]
            low = pl.ds(2 * part * wide, wide)
            high = pl.ds((2 * part + 1) * wide, wide)
            for k in ORDER:
                for q in range(4):
                    if (k, q) != (0, 0):
                        self.main[part, k, q].wait_recv()
                block = self.fin[part, k].astype(F32)
                if k == 0:
                    own = self.out[part, 0:1].astype(F32)
                    block = jnp.concatenate([own, block[1:4]], axis=0)
                block = block.reshape(4, 2, 8, wide)
                rows = pl.ds(PLACE[k] * 32, 32)
                ret[rows, low] = block[:, 0].reshape(32, wide).astype(BF)
                ret[rows, high] = block[:, 1].reshape(32, wide).astype(BF)
            if part == 0:
                self.e_last.wait_recv()
            own, other = self.etot[part, 0].astype(F32), self.ein[part].astype(F32)
            ret[256:272, low] = jnp.concatenate([own[0:8], other[0:8]], axis=0).astype(BF)
            ret[256:272, high] = jnp.concatenate([own[8:16], other[8:16]], axis=0).astype(BF)

    dis_a = Dispatch(send1_a, rx_a, esend_a, emine_a, epart_a, unpack_a)
    dis_b = Dispatch(send1_b, rx_b, esend_b, emine_b, epart_b, unpack_b)
    ret_a = Return(out_a, epin_a, chain_a, etot_a, ein_a, fin_a)
    ret_b = Return(out_b, epin_b, chain_b, etot_b, ein_b, fin_b)
    cut = chunks(6)
    tiles = ff // TILE
    step = min(512, width // PARTS_A)

    routing(1, dd_b, ddt_b, hot_b)
    gates(1, gates_b)
    prepare(hid_b, gates_b, grad_b)
    pack(dd_b, send1_b, rx_b, emine_b, esend_b, columns(nn, 0), columns(gg, 0), width)
    pl.semaphore_wait(barrier, len(greeted))
    dis_b.start_extra()
    dis_b.launch(cut[0])

    routing(0, dd_a, ddt_a, hot_a)
    gates(0, gates_a)
    prepare(hid_a, gates_a, None)
    pack(dd_a, send1_a, rx_a, emine_a, esend_a, columns(nn, 0), columns(nn, half), half)
    ret[272:384, :] = jnp.zeros((112, width), BF)

    dis_b.extra(1)
    dis_a.start_extra()
    dis_b.launch(cut[1])
    for h in range(2, 6):
        dis_b.extra(h)
        dis_a.extra(h - 1)
        dis_b.launch(cut[h])
    dis_a.launch(BLOCKS[:10])
    dis_a.extra(5)
    dis_a.launch(BLOCKS[10:])

    dis_b.collect()
    for copy in weights:
        copy.wait()
    run(backward_units, 0, tiles)
    run(backward_out, 0, half // TILE)
    cut = chunks(4)
    ret_b.swap()
    ret_b.launch(0, cut[0])
    ret_b.extra(1)
    ret_b.launch(0, cut[1])
    dis_a.collect()
    ret_b.extra(2)
    ret_b.launch(0, cut[2])
    run(forward_units, 0, tiles)
    ret_b.extra(3)
    ret_b.launch(0, cut[3])
    for part in range(PARTS_A):
        run(forward_out(part), 0, out_a.shape[3] // TILE)
    ret_b.extra(4)
    ret_a.swap()
    ret_a.launch(0, cut[0])
    ret_a.extra(1)
    ret_a.launch(0, cut[1])
    ret_b.finish_extra()
    ret_a.extra(2)
    ret_a.launch(0, cut[2])
    ret_a.extra(3)
    ret_a.launch(0, cut[3])
    ret_a.extra(4)
    for part in range(1, PARTS_A):
        ret_a.launch(part, BLOCKS)

    ret_b.collect(0)

    @pl.loop(0, width // step)
    def _(i):
        cols = pl.ds(pl.multiple_of(i * step, step), step)
        moved = dot(ddt_b[...], ret[:, cols])
        dnorm[:, cols] = moved[0:tokens] + moved[tokens:]

    @pl.loop(0, tokens // 16)
    def _(i):
        rows = pl.ds(pl.multiple_of(i * 16, 16), 16)
        values = hid_b[rows, :].astype(F32)
        r = inverse_norm(values)
        scaled = dnorm[rows, :] * gain_ref[...]
        inner = jnp.mean(values * scaled, axis=-1, keepdims=True)
        grown = grad_b[rows, :].astype(F32) + r * scaled - values * (r * r * r * inner)
        pipe_b[rows, :] = grown.astype(BF)

    to_prev = describe(pipe_b, prev_ref, pipe_prev)
    if pipes > 1:
        @pl.when(pipe > 0)
        def _():
            to_prev.start()

    ret_a.finish_extra()
    to_next = []
    wide = width // PARTS_A
    for part in range(PARTS_A):
        ret_a.collect(part)

        @pl.loop(0, wide // step)
        def _(i):
            cols = pl.ds(pl.multiple_of(part * wide + i * step, step), step)
            moved = dot(ddt_a[...], ret[:, cols])
            summed = gates_a[0, :, 0:1] * moved[0:tokens] + gates_a[1, :, 0:1] * moved[tokens:]
            pipe_a[:, cols] = (hid_a[:, cols].astype(F32) + summed).astype(BF)

        cols = pl.ds(part * wide, wide)
        copy = describe(pipe_a.at[:, cols], next_ref.at[:, cols], pipe_next)
        to_next.append(copy)
        if pipes > 1:
            @pl.when(pipe < pipes - 1)
            def _():
                copy.start()

    @pl.when(pipe == 0)
    def _():
        next_ref[...] = jnp.zeros(next_ref.shape, BF)

    @pl.when(pipe == pipes - 1)
    def _():
        prev_ref[...] = jnp.zeros(prev_ref.shape, BF)

    for copy in sent:
        copy.wait_send()
    if pipes > 1:
        @pl.when(pipe < pipes - 1)
        def _():
            to_prev.wait_recv()
            for copy in to_next:
                copy.wait_send()

        @pl.when(pipe > 0)
        def _():
            to_prev.wait_send()
            for copy in to_next:
                copy.wait_recv()


def hand_over(first, second, first_out, second_out):
    first_out[...] = first[...]
    second_out[...] = second[...]


def scratch(tokens, width, ff):
    half = width // 2
    vmem = pltpu.VMEM
    part = half // PARTS_A
    shapes = [
        ((width, ff), BF), ((width, ff), BF), ((ff, width), BF),
        ((2 * tokens, width), BF), ((2 * tokens, width), BF),
        ((384, 2 * tokens), BF), ((384, 2 * tokens), BF),
        ((2 * tokens, 384), BF), ((2 * tokens, 384), BF),
        ((32, TILE), F32), ((32, TILE), F32),
        ((2, tokens, tokens), F32), ((2, tokens, tokens), F32),
        ((8, 4, 16, half), BF), ((8, 4, 16, width), BF),
        ((8, 4, 16, half), BF), ((8, 4, 16, width), BF),
        ((16, half), BF), ((16, width), BF),
        ((8, 2, 16, half), BF), ((8, 2, 16, width), BF),
        ((8, 2, 16, half), BF), ((8, 2, 16, width), BF),
        ((512, width), BF), ((512, width), BF), ((512, width), BF),
        ((512, ff), BF), ((512, ff), BF),
        ((PARTS_A, 64, 16, part), BF), ((1, 64, 16, half), BF),
        ((PARTS_A, 16, 16, part), BF), ((1, 16, 16, half), BF),
        ((7, PARTS_A, 2, 16, part), BF), ((7, 1, 2, 16, half), BF),
        ((PARTS_A, 2, 16, part), BF), ((1, 2, 16, half), BF),
        ((PARTS_A, 16, part), BF), ((1, 16, half), BF),
        ((PARTS_A, 8, 4, 16, part), BF), ((1, 8, 4, 16, half), BF),
        ((384, width), BF), ((tokens, width), F32),
        ((tokens, width), BF), ((tokens, width), BF),
    ]
    messages = 256
    return [vmem(shape, kind) for shape, kind in shapes] + [
        pltpu.SemaphoreType.DMA((messages,)),
        pltpu.SemaphoreType.DMA((messages,)),
        pltpu.SemaphoreType.DMA((3,)),
    ]


def per_device(
    hidden_a, expert_ids_a, router_probs_a, hidden_b, expert_ids_b, router_probs_b,
    grad_out_b, norm_gain, w_gate, w_up, w_down,
):
    tokens, width = hidden_a.shape[1:]
    ff = w_gate.shape[3]
    ids = jnp.swapaxes(jnp.concatenate([expert_ids_a, expert_ids_b], axis=0), 1, 2)
    probs = jnp.swapaxes(jnp.concatenate([router_probs_a, router_probs_b], axis=0), 1, 2)
    inside = pl.BlockSpec(memory_space=pltpu.VMEM)
    outside = pl.BlockSpec(memory_space=pl.ANY)
    result = jax.ShapeDtypeStruct((tokens, width), BF)
    rows = 512
    next_hidden, grad_before = pl.pallas_call(
        kernel,
        out_shape=(result, result),
        in_specs=[inside] * 6 + [outside] * 3,
        out_specs=(inside, inside),
        scratch_shapes=scratch(tokens, width, ff),
        compiler_params=pltpu.CompilerParams(
            collective_id=0, has_side_effects=True, vmem_limit_bytes=60 * 1024 * 1024
        ),
        cost_estimate=pl.CostEstimate(
            flops=2 * rows * width * ff * 8, bytes_accessed=6 * width * ff, transcendentals=0
        ),
    )(
        ids, probs, hidden_a[0], hidden_b[0], grad_out_b[0],
        norm_gain, w_gate[0, 0], w_up[0, 0], w_down[0, 0],
    )
    next_hidden, grad_before = pl.pallas_call(
        hand_over,
        out_shape=(result, result),
        in_specs=[inside] * 2,
        out_specs=(inside, inside),
    )(next_hidden, grad_before)
    return next_hidden[None], grad_before[None]


def solution(mesh):
    in_specs = (
        P("pipe", "expert", None),
        P("pipe", "expert", None),
        P("pipe", "expert", None),
        P("pipe", "expert", None),
        P("pipe", "expert", None),
        P("pipe", "expert", None),
        P("pipe", "expert", None),
        P("pipe", None),
        P("pipe", "expert", None, None),
        P("pipe", "expert", None, None),
        P("pipe", "expert", None, None),
    )
    out_specs = (P("pipe", "expert", None), P("pipe", "expert", None))
    return jax.shard_map(
        per_device, mesh=mesh, in_specs=in_specs, out_specs=out_specs, check_vma=False
    )
```

time: 203 us -> 181 us (0.89)
  the two profiles are of different devices: /device:TPU:6 before, /device:TPU:12 now
where the time goes in v1:
time: 181 us
  Pallas kernels  178 us (98%)
  other arithmetic  2.6 us (1%)
    pallas_call x1, Pallas kernels, per_device(): pl.pallas_call(kernel, out_shape=(result, result), in_specs=[inside] * 6...  176 us

profile of v1, /device:TPU:12, one launch (start us, length us, event | category | flops | bytes accessed | tf_op | source)
XLA Modules:
  0.0 181.0 jit_solution(14487046654254167237)
XLA Ops:
  0.6 1.3 add_bitcast_fusion.ids_ref
  1.9 1.3 maximum_bitcast_fusion.probs_ref
  3.2 175.5 %shard_map.122 = (bf16[128,2048]{1,0:T(8,128)(2,1)}, bf16[128,2048]{1,0:T(8,128)(2,1)}) custom-call(s32[2,8,128]{2,1,0:T(8,128)} %add_bitcast_fusion.ids_ref, f32[2,8,128]{2,1,0:T(8,128)} %maximum_bitcast_fusion.probs_ref, bf16[128,2048]{1,0:T(8,128)(2,1)} %bitcast.15, bf16[128,2048]{1,0:T(8,128)(2,1)} %bitcast.16, bf16[128,2048]{1,0:T(8,128)(2,1)} %bitcast.17, ...), custom_call_target="tpu_custom_call" | custom-call | flops 12884901888 | bytes 9437184 | tf_op jit(solution)/shard_map/pallas_call | solution.py:560
  178.8 2.2 %shard_map.123 = (bf16[128,2048]{1,0:T(8,128)(2,1)}, bf16[128,2048]{1,0:T(8,128)(2,1)}) custom-call(bf16[128,2048]{1,0:T(8,128)(2,1)} %get-tuple-element.6.first, bf16[128,2048]{1,0:T(8,128)(2,1)} %get-tuple-element.7.second), custom_call_target="tpu_custom_call" | custom-call | tf_op jit(solution)/shard_map/pallas_call | solution.py:576

commit v2 on v1

--- a/solution.py
+++ b/solution.py
@@ -13,8 +13,9 @@
 ORDER = (4, 3, 5, 2, 6, 1, 7, 0)
 PLACE = {k: s for s, k in enumerate(ORDER)}
 TILE = 256
-PARTS_A = 2
+PARTS_A = 4
 BLOCKS = [(k, q) for k in ORDER for q in (2, 3, 0, 1) if (k, q) != (0, 0)]
+SEMAPHORES = 91
 EXTRA_HOPS = {"L": 4, "S": 3}
 
 
@@ -32,13 +33,14 @@
 
 
 def kernel(
-    ids_ref, probs_ref, hid_a, hid_b, grad_b, gain_ref, wg_hbm, wu_hbm, wd_hbm,
+    ids_a_hbm, ids_b_hbm, probs_a_hbm, probs_b_hbm, hid_a_hbm, hid_b_hbm, grad_b_hbm, gain_hbm,
+    wg_hbm, wu_hbm, wd_hbm,
     next_ref, prev_ref,
-    wg, wu, wd, nn, gg, dd_a, dd_b, ddt_a, ddt_b, hot_a, hot_b, gates_a, gates_b,
+    ids_a, ids_b, probs_a, probs_b, hid_a, hid_b, grad_b, gain_ref, wg, wu, wd, nn, gg, dd_a, dd_b, ddt_a, ddt_b, hot_a, hot_b, gates_a, gates_b,
     send1_a, send1_b, rx_a, rx_b, esend_a, esend_b, emine_a, emine_b, epart_a, epart_b,
     x_a, x_b, s_b, hid1, hid2, out_a, out_b, epin_a, epin_b,
     chain_a, chain_b, etot_a, etot_b, ein_a, ein_b, fin_a, fin_b,
-    ret, dnorm, pipe_a, pipe_b, send_sems, recv_sems, local_sems,
+    ret, dnorm, pipe_a, pipe_b, sems,
 ):
     pipe = lax.axis_index("pipe")
     pipes = lax.axis_size("pipe")
@@ -73,27 +75,22 @@
     pipe_prev = {"pipe": lax.rem(pipe + pipes - 1, pipes)}
 
     used = [0]
-    sent = []
-
-    def describe(src, dst, target):
-        i = used[0]
-        used[0] += 1
-        return pltpu.make_async_remote_copy(
-            src_ref=src, dst_ref=dst, send_sem=send_sems.at[i], recv_sem=recv_sems.at[i],
-            device_id=target, device_id_type=MESH,
+    unwaited = []
+
+    def semaphores(count):
+        first = used[0]
+        used[0] += count
+        return [sems.at[first + i] for i in range(count)]
+
+    def wait_for(ref, sem):
+        pltpu.make_async_copy(ref, ref, sem).wait()
+
+    def send(src, dst, where, send_sem, recv_sem):
+        copy = pltpu.make_async_remote_copy(
+            src_ref=src, dst_ref=dst, send_sem=send_sem, recv_sem=recv_sem,
+            device_id=where, device_id_type=MESH,
         )
-
-    def send(src, dst, target):
-        copy = describe(src, dst, target)
         copy.start()
-        sent.append(copy)
-        return copy
-
-    weights = []
-    for i, (src, dst) in enumerate(((wg_hbm, wg), (wu_hbm, wu), (wd_hbm, wd))):
-        copy = pltpu.make_async_copy(src, dst, local_sems.at[i])
-        copy.start()
-        weights.append(copy)
 
     barrier = pltpu.get_barrier_semaphore()
     greeted = [target(k, q) for k, q in BLOCKS]
@@ -102,8 +99,24 @@
     for other in greeted:
         pl.semaphore_signal(barrier, inc=1, device_id=other, device_id_type=MESH)
 
-    def routing(which, dd, ddt, hot):
-        ids = ids_ref[which]
+    def fetch(src, dst):
+        copy = pltpu.make_async_copy(src, dst, semaphores(1)[0])
+        copy.start()
+        return copy
+
+    got_b = [
+        fetch(*pair) for pair in (
+            (ids_b_hbm, ids_b), (probs_b_hbm, probs_b), (gain_hbm, gain_ref),
+            (hid_b_hbm, hid_b), (grad_b_hbm, grad_b),
+        )
+    ]
+    got_a = [
+        fetch(*pair) for pair in ((ids_a_hbm, ids_a), (probs_a_hbm, probs_a), (hid_a_hbm, hid_a))
+    ]
+    weights = [fetch(*pair) for pair in ((wg_hbm, wg), (wu_hbm, wu), (wd_hbm, wd))]
+
+    def routing(ids_ref, dd, ddt, hot):
+        ids = ids_ref[...]
         j = lax.broadcasted_iota(jnp.int32, (32, tokens), 0)
         q = j & 3
         s = j >> 2
@@ -144,8 +157,8 @@
 
     xf = x.astype(F32)
 
-    def gates(which, gate):
-        probs = probs_ref[which]
+    def gates(probs_ref, gate):
+        probs = probs_ref[...]
         weight = probs / jnp.sum(probs, axis=0, keepdims=True)
         first, second = weight[0:1, :], weight[1:2, :]
         for i, row in enumerate(
@@ -196,31 +209,42 @@
         def __init__(self, send1, rx, esend, emine, epart, unpack):
             self.send1, self.rx, self.esend, self.emine = send1, rx, esend, emine
             self.epart, self.unpack = epart, unpack
-            self.main, self.hop, self.part = {}, {}, {}
+            self.main_sem = semaphores(RING)
+            self.hop_sem = {"L": semaphores(4), "S": semaphores(3)}
+            self.first_sem, self.part_sem = semaphores(2)
+            self.sent_first, self.sent_hop, self.sent_part = semaphores(3)
+            self.sent_far, self.sent_near = semaphores(2)
+            unwaited.extend([
+                (rx.at[pl.ds(1, 7)], self.sent_far), (rx.at[0, pl.ds(1, 3)], self.sent_near),
+                (esend, self.sent_first), (emine.at[pl.ds(0, 7)], self.sent_hop),
+                (emine, self.sent_part),
+            ])
 
         def launch(self, blocks):
             for k, q in blocks:
-                self.main[k, q] = send(
-                    self.send1.at[PLACE[k], q], self.rx.at[k, q], target(k, q)
+                send(
+                    self.send1.at[PLACE[k], q], self.rx.at[k, q], target(k, q),
+                    self.sent_far if k else self.sent_near, self.main_sem[k],
                 )
 
         def start_extra(self):
-            self.e_first = send(self.esend, self.emine.at[0, 1], partner[2])
+            send(self.esend, self.emine.at[0, 1], partner[2], self.sent_first, self.first_sem)
 
         def swap_extra(self, k):
-            self.part[k] = send(self.emine.at[k], self.epart.at[k], partner[1])
+            send(self.emine.at[k], self.epart.at[k], partner[1], self.sent_part, self.part_sem)
 
         def extra(self, h):
             if h == 1:
-                self.e_first.wait_recv()
+                wait_for(self.emine.at[0, 1], self.first_sem)
             for way, last in EXTRA_HOPS.items():
                 if 1 < h <= last + 1:
-                    self.hop[way, h - 1].wait_recv()
+                    wait_for(self.emine.at[0], self.hop_sem[way][h - 2])
                 if h <= last:
                     a, b = (h - 1, h) if way == "L" else ((9 - h) % RING, RING - h)
-                    self.hop[way, h] = send(
+                    send(
                         self.emine.at[a], self.emine.at[b],
                         long_way if way == "L" else short_way,
+                        self.sent_hop, self.hop_sem[way][h - 1],
                     )
             if h <= 5:
                 for k in {h - 1, (9 - h) % RING} if h <= 4 else {4}:
@@ -228,13 +252,12 @@
 
         def collect(self):
             for k in ORDER:
-                for q in range(4):
-                    if (k, q) != (0, 0):
-                        self.main[k, q].wait_recv()
+                arrived = self.rx.at[k] if k else self.rx.at[0, pl.ds(1, 3)]
+                wait_for(arrived, self.main_sem[k])
                 self.unpack(self.rx.at[k], k * 32)
-            for k in (0, 1, 7, 2, 6, 3, 5, 4):
+            wait_for(self.epart, self.part_sem)
+            for k in range(RING):
                 self.unpack(self.emine.at[k], 256 + k * 16)
-                self.part[k].wait_recv()
                 self.unpack(self.epart.at[k], 384 + k * 16)
 
     def unpack_b(src, row):
@@ -307,66 +330,75 @@
         def __init__(self, out, epin, chain, etot, ein, fin):
             self.out, self.epin, self.chain = out, epin, chain
             self.etot, self.ein, self.fin = etot, ein, fin
-            self.main, self.hop = {}, {}
+            self.main_sem = semaphores(out.shape[0])
+            self.hop_sem = {"L": semaphores(4), "S": semaphores(3)}
+            self.swap_sem, self.last_sem = semaphores(2)
+            self.sent_main, self.sent_hop, self.sent_swap, self.sent_last = semaphores(4)
+            unwaited.extend([
+                (fin, self.sent_main), (chain, self.sent_hop), (epin, self.sent_swap),
+                (ein, self.sent_last),
+            ])
 
         def launch(self, part, blocks):
             for k, q in blocks:
-                self.main[part, k, q] = send(
-                    self.out.at[part, 4 * k + q], self.fin.at[part, k, q], source(k, q)
+                send(
+                    self.out.at[part, 4 * k + q], self.fin.at[part, 4 * k + q - 1], source(k, q),
+                    self.sent_main, self.main_sem[part],
                 )
 
         def swap(self):
-            self.swapped = send(self.out.at[:, pl.ds(48, 16)], self.epin, partner[1])
+            send(
+                self.out.at[:, pl.ds(48, 16)], self.epin, partner[1],
+                self.sent_swap, self.swap_sem,
+            )
+
+        def hop(self, way, h, src, dst):
+            send(
+                src, dst, short_way if way == "L" else long_way,
+                self.sent_hop, self.hop_sem[way][h - 1],
+            )
 
         def extra(self, h):
             if h == 1:
-                self.swapped.wait_recv()
+                wait_for(self.epin, self.swap_sem)
                 mine = self.out[:, 32:48].astype(F32)
                 self.epin[...] = (mine + self.epin[...].astype(F32)).astype(BF)
-                self.hop["L", 1] = send(
-                    self.epin.at[:, pl.ds(8, 2)], self.chain.at[0], short_way
-                )
-                self.hop["S", 1] = send(
-                    self.epin.at[:, pl.ds(10, 2)], self.chain.at[4], long_way
-                )
+                self.hop("L", 1, self.epin.at[:, pl.ds(8, 2)], self.chain.at[0])
+                self.hop("S", 1, self.epin.at[:, pl.ds(10, 2)], self.chain.at[4])
                 return
             for way, last in EXTRA_HOPS.items():
                 if h > last:
                     continue
-                self.hop[way, h - 1].wait_recv()
                 k, at = (5 - h, h - 2) if way == "L" else (4 + h, 2 + h)
+                wait_for(self.chain.at[at], self.hop_sem[way][h - 2])
                 mine = self.epin[:, 2 * k:2 * k + 2].astype(F32)
                 self.chain[at] = (self.chain[at].astype(F32) + mine).astype(BF)
-                self.hop[way, h] = send(
-                    self.chain.at[at], self.chain.at[at + 1],
-                    short_way if way == "L" else long_way,
-                )
+                self.hop(way, h, self.chain.at[at], self.chain.at[at + 1])
 
         def finish_extra(self):
-            self.hop["L", 4].wait_recv()
-            self.hop["S", 3].wait_recv()
+            wait_for(self.chain.at[3], self.hop_sem["L"][3])
+            wait_for(self.chain.at[6], self.hop_sem["S"][2])
             total = self.epin[:, 0:2].astype(F32) + self.chain[3].astype(F32)
             self.etot[...] = (total + self.chain[6].astype(F32)).astype(BF)
-            self.e_last = send(self.etot.at[:, 1], self.ein, partner[2])
+            send(self.etot.at[:, 1], self.ein, partner[2], self.sent_last, self.last_sem)
 
         def collect(self, part):
             wide = self.out.shape[3]
             low = pl.ds(2 * part * wide, wide)
             high = pl.ds((2 * part + 1) * wide, wide)
-            for k in ORDER:
-                for q in range(4):
-                    if (k, q) != (0, 0):
-                        self.main[part, k, q].wait_recv()
-                block = self.fin[part, k].astype(F32)
+            wait_for(self.fin.at[part], self.main_sem[part])
+            for k in range(RING):
                 if k == 0:
                     own = self.out[part, 0:1].astype(F32)
-                    block = jnp.concatenate([own, block[1:4]], axis=0)
+                    block = jnp.concatenate([own, self.fin[part, 0:3].astype(F32)], axis=0)
+                else:
+                    block = self.fin[part, 4 * k - 1:4 * k + 3].astype(F32)
                 block = block.reshape(4, 2, 8, wide)
                 rows = pl.ds(PLACE[k] * 32, 32)
                 ret[rows, low] = block[:, 0].reshape(32, wide).astype(BF)
                 ret[rows, high] = block[:, 1].reshape(32, wide).astype(BF)
             if part == 0:
-                self.e_last.wait_recv()
+                wait_for(self.ein, self.last_sem)
             own, other = self.etot[part, 0].astype(F32), self.ein[part].astype(F32)
             ret[256:272, low] = jnp.concatenate([own[0:8], other[0:8]], axis=0).astype(BF)
             ret[256:272, high] = jnp.concatenate([own[8:16], other[8:16]], axis=0).astype(BF)
@@ -379,19 +411,37 @@
     tiles = ff // TILE
     step = min(512, width // PARTS_A)
 
-    routing(1, dd_b, ddt_b, hot_b)
-    gates(1, gates_b)
+    for copy in got_b:
+        copy.wait()
+    routing(ids_b, dd_b, ddt_b, hot_b)
+    gates(probs_b, gates_b)
     prepare(hid_b, gates_b, grad_b)
     pack(dd_b, send1_b, rx_b, emine_b, esend_b, columns(nn, 0), columns(gg, 0), width)
     pl.semaphore_wait(barrier, len(greeted))
     dis_b.start_extra()
     dis_b.launch(cut[0])
 
-    routing(0, dd_a, ddt_a, hot_a)
-    gates(0, gates_a)
+    for copy in got_a:
+        copy.wait()
+    routing(ids_a, dd_a, ddt_a, hot_a)
+    gates(probs_a, gates_a)
     prepare(hid_a, gates_a, None)
     pack(dd_a, send1_a, rx_a, emine_a, esend_a, columns(nn, 0), columns(nn, half), half)
     ret[272:384, :] = jnp.zeros((112, width), BF)
+    prev_sent, prev_got, next_sent, next_got, zero_sem = semaphores(5)
+
+    def blank(ref):
+        nn[0:tokens, :] = jnp.zeros((tokens, width), BF)
+        pltpu.make_async_copy(nn.at[pl.ds(0, tokens)], ref, zero_sem).start()
+        pltpu.make_async_copy(nn.at[pl.ds(0, tokens)], ref, zero_sem).wait()
+
+    @pl.when(pipe == 0)
+    def _():
+        blank(next_ref)
+
+    @pl.when(pipe == pipes - 1)
+    def _():
+        blank(prev_ref)
 
     dis_b.extra(1)
     dis_a.start_extra()
@@ -409,30 +459,21 @@
         copy.wait()
     run(backward_units, 0, tiles)
     run(backward_out, 0, half // TILE)
-    cut = chunks(4)
     ret_b.swap()
-    ret_b.launch(0, cut[0])
-    ret_b.extra(1)
-    ret_b.launch(0, cut[1])
+    ret_b.launch(0, BLOCKS[:8])
     dis_a.collect()
-    ret_b.extra(2)
-    ret_b.launch(0, cut[2])
+    ret_b.launch(0, BLOCKS[8:14])
     run(forward_units, 0, tiles)
-    ret_b.extra(3)
-    ret_b.launch(0, cut[3])
     for part in range(PARTS_A):
         run(forward_out(part), 0, out_a.shape[3] // TILE)
-    ret_b.extra(4)
     ret_a.swap()
-    ret_a.launch(0, cut[0])
-    ret_a.extra(1)
-    ret_a.launch(0, cut[1])
+    for h, (start, end) in enumerate(((14, 20), (20, 26), (26, 31), (31, 31))):
+        ret_b.extra(h + 1)
+        ret_a.extra(h + 1)
+        ret_b.launch(0, BLOCKS[start:end])
+    ret_a.launch(0, BLOCKS)
     ret_b.finish_extra()
-    ret_a.extra(2)
-    ret_a.launch(0, cut[2])
-    ret_a.extra(3)
-    ret_a.launch(0, cut[3])
-    ret_a.extra(4)
+    ret_a.finish_extra()
     for part in range(1, PARTS_A):
         ret_a.launch(part, BLOCKS)
 
@@ -454,14 +495,11 @@
         grown = grad_b[rows, :].astype(F32) + r * scaled - values * (r * r * r * inner)
         pipe_b[rows, :] = grown.astype(BF)
 
-    to_prev = describe(pipe_b, prev_ref, pipe_prev)
     if pipes > 1:
         @pl.when(pipe > 0)
         def _():
-            to_prev.start()
-
-    ret_a.finish_extra()
-    to_next = []
+            send(pipe_b, prev_ref, pipe_prev, prev_sent, prev_got)
+
     wide = width // PARTS_A
     for part in range(PARTS_A):
         ret_a.collect(part)
@@ -474,35 +512,23 @@
             pipe_a[:, cols] = (hid_a[:, cols].astype(F32) + summed).astype(BF)
 
         cols = pl.ds(part * wide, wide)
-        copy = describe(pipe_a.at[:, cols], next_ref.at[:, cols], pipe_next)
-        to_next.append(copy)
         if pipes > 1:
             @pl.when(pipe < pipes - 1)
             def _():
-                copy.start()
-
-    @pl.when(pipe == 0)
-    def _():
-        next_ref[...] = jnp.zeros(next_ref.shape, BF)
-
-    @pl.when(pipe == pipes - 1)
-    def _():
-        prev_ref[...] = jnp.zeros(prev_ref.shape, BF)
-
-    for copy in sent:
-        copy.wait_send()
+                send(pipe_a.at[:, cols], next_ref.at[:, cols], pipe_next, next_sent, next_got)
+
+    for ref, sem in unwaited:
+        wait_for(ref, sem)
     if pipes > 1:
         @pl.when(pipe < pipes - 1)
         def _():
-            to_prev.wait_recv()
-            for copy in to_next:
-                copy.wait_send()
+            wait_for(prev_ref, prev_got)
+            wait_for(pipe_a, next_sent)
 
         @pl.when(pipe > 0)
         def _():
-            to_prev.wait_send()
-            for copy in to_next:
-                copy.wait_recv()
+            wait_for(pipe_b, prev_sent)
+            wait_for(next_ref, next_got)
 
 
 def hand_over(first, second, first_out, second_out):
@@ -533,15 +559,16 @@
         ((7, PARTS_A, 2, 16, part), BF), ((7, 1, 2, 16, half), BF),
         ((PARTS_A, 2, 16, part), BF), ((1, 2, 16, half), BF),
         ((PARTS_A, 16, part), BF), ((1, 16, half), BF),
-        ((PARTS_A, 8, 4, 16, part), BF), ((1, 8, 4, 16, half), BF),
+        ((PARTS_A, 31, 16, part), BF), ((1, 31, 16, half), BF),
         ((384, width), BF), ((tokens, width), F32),
         ((tokens, width), BF), ((tokens, width), BF),
     ]
-    messages = 256
-    return [vmem(shape, kind) for shape, kind in shapes] + [
-        pltpu.SemaphoreType.DMA((messages,)),
-        pltpu.SemaphoreType.DMA((messages,)),
-        pltpu.SemaphoreType.DMA((3,)),
+    arguments = [
+        ((8, tokens), jnp.int32), ((8, tokens), jnp.int32), ((8, tokens), F32), ((8, tokens), F32),
+        ((tokens, width), BF), ((tokens, width), BF), ((tokens, width), BF), ((1, width), F32),
+    ]
+    return [vmem(shape, kind) for shape, kind in arguments + shapes] + [
+        pltpu.SemaphoreType.DMA((SEMAPHORES,))
     ]
 
 
@@ -551,8 +578,10 @@
 ):
     tokens, width = hidden_a.shape[1:]
     ff = w_gate.shape[3]
-    ids = jnp.swapaxes(jnp.concatenate([expert_ids_a, expert_ids_b], axis=0), 1, 2)
-    probs = jnp.swapaxes(jnp.concatenate([router_probs_a, router_probs_b], axis=0), 1, 2)
+    small = [
+        jnp.swapaxes(value[0], 0, 1)
+        for value in (expert_ids_a, expert_ids_b, router_probs_a, router_probs_b)
+    ]
     inside = pl.BlockSpec(memory_space=pltpu.VMEM)
     outside = pl.BlockSpec(memory_space=pl.ANY)
     result = jax.ShapeDtypeStruct((tokens, width), BF)
@@ -560,8 +589,8 @@
     next_hidden, grad_before = pl.pallas_call(
         kernel,
         out_shape=(result, result),
-        in_specs=[inside] * 6 + [outside] * 3,
-        out_specs=(inside, inside),
+        in_specs=[outside] * 11,
+        out_specs=(outside, outside),
         scratch_shapes=scratch(tokens, width, ff),
         compiler_params=pltpu.CompilerParams(
             collective_id=0, has_side_effects=True, vmem_limit_bytes=60 * 1024 * 1024
@@ -570,7 +599,7 @@
             flops=2 * rows * width * ff * 8, bytes_accessed=6 * width * ff, transcendentals=0
         ),
     )(
-        ids, probs, hidden_a[0], hidden_b[0], grad_out_b[0],
+        *small, hidden_a[0], hidden_b[0], grad_out_b[0],
         norm_gain, w_gate[0, 0], w_up[0, 0], w_down[0, 0],
     )
     next_hidden, grad_before = pl.pallas_call(

time: 181 us -> 162 us (0.90)
  the two profiles are of different devices: /device:TPU:12 before, /device:TPU:6 now
where the time goes in v2:
time: 162 us
  Pallas kernels  161 us (99%)
    pallas_call x1, Pallas kernels, per_device(): pl.pallas_call(kernel, out_shape=(result, result), in_specs=[outside] * 1...  159 us

profile of v2, /device:TPU:6, one launch (start us, length us, event | category | flops | bytes accessed | tf_op | source)
XLA Modules:
  0.0 161.9 jit_solution(17354169589764794928)
XLA Ops:
  0.6 159.0 %shard_map.122 = (bf16[128,2048]{1,0:T(8,128)(2,1)}, bf16[128,2048]{1,0:T(8,128)(2,1)}) custom-call(s32[8,128]{1,0:T(8,128)} %bitcast.28, s32[8,128]{1,0:T(8,128)} %bitcast.29, f32[8,128]{1,0:T(8,128)} %bitcast.30, f32[8,128]{1,0:T(8,128)} %bitcast.31, bf16[128,2048]{1,0:T(8,128)(2,1)} %bitcast.23, bf16[128,2048]{1,0:T(8,128)(2,1)} %bitcast.24, ...), custom_call_target="tpu_custom_call" | custom-call | flops 12884901888 | bytes 9437184 | tf_op jit(solution)/shard_map/pallas_call | solution.py:589
  159.7 2.2 %shard_map.123 = (bf16[128,2048]{1,0:T(8,128)(2,1)}, bf16[128,2048]{1,0:T(8,128)(2,1)}) custom-call(bf16[128,2048]{1,0:T(8,128)(2,1)} %get-tuple-element.6.first, bf16[128,2048]{1,0:T(8,128)(2,1)} %get-tuple-element.7.second), custom_call_target="tpu_custom_call" | custom-call | tf_op jit(solution)/shard_map/pallas_call | solution.py:605

commit v3 on v2

--- a/solution.py
+++ b/solution.py
@@ -13,9 +13,9 @@
 ORDER = (4, 3, 5, 2, 6, 1, 7, 0)
 PLACE = {k: s for s, k in enumerate(ORDER)}
 TILE = 256
-PARTS_A = 4
+PARTS_A = 8
 BLOCKS = [(k, q) for k in ORDER for q in (2, 3, 0, 1) if (k, q) != (0, 0)]
-SEMAPHORES = 91
+SEMAPHORES = 96
 EXTRA_HOPS = {"L": 4, "S": 3}
 
 
@@ -38,7 +38,7 @@
     next_ref, prev_ref,
     ids_a, ids_b, probs_a, probs_b, hid_a, hid_b, grad_b, gain_ref, wg, wu, wd, nn, gg, dd_a, dd_b, ddt_a, ddt_b, hot_a, hot_b, gates_a, gates_b,
     send1_a, send1_b, rx_a, rx_b, esend_a, esend_b, emine_a, emine_b, epart_a, epart_b,
-    x_a, x_b, s_b, hid1, hid2, out_a, out_b, epin_a, epin_b,
+    x_a, x_b, s_b, hid1, hid2, out_a, out_b, oute_a, oute_b, epin_a, epin_b,
     chain_a, chain_b, etot_a, etot_b, ein_a, ein_b, fin_a, fin_b,
     ret, dnorm, pipe_a, pipe_b, sems,
 ):
@@ -292,7 +292,7 @@
         hid1[:, cols] = (d_hidden * up_pre * sigma * (1.0 + gate_pre * (1.0 - sigma))).astype(BF)
         hid2[:, cols] = (d_hidden * gate_pre * sigma).astype(BF)
 
-    def store_out(out, part, hot, i, low, high):
+    def store_out(out, oute, hot, i, low, high):
         valid = jnp.broadcast_to(hot[28:29, :], (256, TILE)) > 8.5
         both = []
         for half_rows in (low, high):
@@ -300,26 +300,28 @@
             both.append(
                 jnp.concatenate([half_rows[0:256], extra], axis=0).reshape(64, 8, TILE)
             )
-        out[part, :, :, tile_at(i)] = jnp.concatenate(both, axis=1).astype(BF)
+        rows = jnp.concatenate(both, axis=1).astype(BF)
+        oute[:, :, tile_at(i)] = rows[32:64]
+        wide = out.shape[3]
+        if out.shape[0] == 1:
+            out[0, :, :, tile_at(i)] = rows[0:32]
+        else:
+            for j in range(TILE // wide):
+                out[i * (TILE // wide) + j] = rows[0:32, :, j * wide:(j + 1) * wide]
 
     def shifted(base, i):
         return pl.ds(pl.multiple_of(base + i * TILE, TILE), TILE)
 
-    def forward_out(part):
-        wide = out_a.shape[3]
-
-        def step(i):
-            low = dot(hid1[...], wd[:, shifted(2 * part * wide, i)])
-            high = dot(hid1[...], wd[:, shifted((2 * part + 1) * wide, i)])
-            store_out(out_a, part, hot_a, i, low, high)
-
-        return step
+    def forward_out(i):
+        low = dot(hid1[...], wd[:, shifted(0, i)])
+        high = dot(hid1[...], wd[:, shifted(half, i)])
+        store_out(out_a, oute_a, hot_a, i, low, high)
 
     def backward_out(i):
         now, later = shifted(0, i), shifted(half, i)
         low = last_dot(hid1[...], wg[now, :]) + last_dot(hid2[...], wu[now, :])
         high = last_dot(hid1[...], wg[later, :]) + last_dot(hid2[...], wu[later, :])
-        store_out(out_b, 0, hot_b, i, low, high)
+        store_out(out_b, oute_b, hot_b, i, low, high)
 
     def run(step, first, last):
         @pl.loop(first, last)
@@ -327,10 +329,11 @@
             step(i)
 
     class Return:
-        def __init__(self, out, epin, chain, etot, ein, fin):
-            self.out, self.epin, self.chain = out, epin, chain
+        def __init__(self, parts, out, oute, epin, chain, etot, ein, fin):
+            self.parts, self.out, self.oute = parts, out, oute
+            self.epin, self.chain = epin, chain
             self.etot, self.ein, self.fin = etot, ein, fin
-            self.main_sem = semaphores(out.shape[0])
+            self.main_sem = semaphores(len(parts))
             self.hop_sem = {"L": semaphores(4), "S": semaphores(3)}
             self.swap_sem, self.last_sem = semaphores(2)
             self.sent_main, self.sent_hop, self.sent_swap, self.sent_last = semaphores(4)
@@ -341,15 +344,15 @@
 
         def launch(self, part, blocks):
             for k, q in blocks:
+                i = 4 * k + q
                 send(
-                    self.out.at[part, 4 * k + q], self.fin.at[part, 4 * k + q - 1], source(k, q),
+                    self.out.at[part, i], self.fin.at[part, i - 1], source(k, q),
                     self.sent_main, self.main_sem[part],
                 )
 
         def swap(self):
             send(
-                self.out.at[:, pl.ds(48, 16)], self.epin, partner[1],
-                self.sent_swap, self.swap_sem,
+                self.oute.at[pl.ds(16, 16)], self.epin, partner[1], self.sent_swap, self.swap_sem
             )
 
         def hop(self, way, h, src, dst):
@@ -361,31 +364,37 @@
         def extra(self, h):
             if h == 1:
                 wait_for(self.epin, self.swap_sem)
-                mine = self.out[:, 32:48].astype(F32)
+                mine = self.oute[0:16].astype(F32)
                 self.epin[...] = (mine + self.epin[...].astype(F32)).astype(BF)
-                self.hop("L", 1, self.epin.at[:, pl.ds(8, 2)], self.chain.at[0])
-                self.hop("S", 1, self.epin.at[:, pl.ds(10, 2)], self.chain.at[4])
+                self.hop("L", 1, self.epin.at[pl.ds(8, 2)], self.chain.at[0])
+                self.hop("S", 1, self.epin.at[pl.ds(10, 2)], self.chain.at[4])
                 return
             for way, last in EXTRA_HOPS.items():
                 if h > last:
                     continue
                 k, at = (5 - h, h - 2) if way == "L" else (4 + h, 2 + h)
                 wait_for(self.chain.at[at], self.hop_sem[way][h - 2])
-                mine = self.epin[:, 2 * k:2 * k + 2].astype(F32)
+                mine = self.epin[2 * k:2 * k + 2].astype(F32)
                 self.chain[at] = (self.chain[at].astype(F32) + mine).astype(BF)
                 self.hop(way, h, self.chain.at[at], self.chain.at[at + 1])
 
         def finish_extra(self):
             wait_for(self.chain.at[3], self.hop_sem["L"][3])
             wait_for(self.chain.at[6], self.hop_sem["S"][2])
-            total = self.epin[:, 0:2].astype(F32) + self.chain[3].astype(F32)
+            total = self.epin[0:2].astype(F32) + self.chain[3].astype(F32)
             self.etot[...] = (total + self.chain[6].astype(F32)).astype(BF)
-            send(self.etot.at[:, 1], self.ein, partner[2], self.sent_last, self.last_sem)
+            send(self.etot.at[1], self.ein, partner[2], self.sent_last, self.last_sem)
+
+        def collect_extra(self):
+            wait_for(self.ein, self.last_sem)
+            own, other = self.etot[0].astype(F32), self.ein[...].astype(F32)
+            ret[256:272, 0:half] = jnp.concatenate([own[0:8], other[0:8]], axis=0).astype(BF)
+            ret[256:272, half:] = jnp.concatenate([own[8:16], other[8:16]], axis=0).astype(BF)
 
         def collect(self, part):
-            wide = self.out.shape[3]
-            low = pl.ds(2 * part * wide, wide)
-            high = pl.ds((2 * part + 1) * wide, wide)
+            start, end = self.parts[part]
+            wide = end - start
+            cols = pl.ds(start, wide)
             wait_for(self.fin.at[part], self.main_sem[part])
             for k in range(RING):
                 if k == 0:
@@ -395,21 +404,17 @@
                     block = self.fin[part, 4 * k - 1:4 * k + 3].astype(F32)
                 block = block.reshape(4, 2, 8, wide)
                 rows = pl.ds(PLACE[k] * 32, 32)
-                ret[rows, low] = block[:, 0].reshape(32, wide).astype(BF)
-                ret[rows, high] = block[:, 1].reshape(32, wide).astype(BF)
-            if part == 0:
-                wait_for(self.ein, self.last_sem)
-            own, other = self.etot[part, 0].astype(F32), self.ein[part].astype(F32)
-            ret[256:272, low] = jnp.concatenate([own[0:8], other[0:8]], axis=0).astype(BF)
-            ret[256:272, high] = jnp.concatenate([own[8:16], other[8:16]], axis=0).astype(BF)
+                ret[rows, cols] = block[:, 0].reshape(32, wide).astype(BF)
+                ret[rows, pl.ds(half + start, wide)] = block[:, 1].reshape(32, wide).astype(BF)
 
     dis_a = Dispatch(send1_a, rx_a, esend_a, emine_a, epart_a, unpack_a)
     dis_b = Dispatch(send1_b, rx_b, esend_b, emine_b, epart_b, unpack_b)
-    ret_a = Return(out_a, epin_a, chain_a, etot_a, ein_a, fin_a)
-    ret_b = Return(out_b, epin_b, chain_b, etot_b, ein_b, fin_b)
+    parts = [(i * half // PARTS_A, (i + 1) * half // PARTS_A) for i in range(PARTS_A)]
+    ret_a = Return(parts, out_a, oute_a, epin_a, chain_a, etot_a, ein_a, fin_a)
+    ret_b = Return([(0, half)], out_b, oute_b, epin_b, chain_b, etot_b, ein_b, fin_b)
     cut = chunks(6)
     tiles = ff // TILE
-    step = min(512, width // PARTS_A)
+    step = min(512, half)
 
     for copy in got_b:
         copy.wait()
@@ -464,8 +469,7 @@
     dis_a.collect()
     ret_b.launch(0, BLOCKS[8:14])
     run(forward_units, 0, tiles)
-    for part in range(PARTS_A):
-        run(forward_out(part), 0, out_a.shape[3] // TILE)
+    run(forward_out, 0, half // TILE)
     ret_a.swap()
     for h, (start, end) in enumerate(((14, 20), (20, 26), (26, 31), (31, 31))):
         ret_b.extra(h + 1)
@@ -474,9 +478,10 @@
     ret_a.launch(0, BLOCKS)
     ret_b.finish_extra()
     ret_a.finish_extra()
-    for part in range(1, PARTS_A):
+    for part in range(1, len(parts)):
         ret_a.launch(part, BLOCKS)
 
+    ret_b.collect_extra()
     ret_b.collect(0)
 
     @pl.loop(0, width // step)
@@ -500,22 +505,22 @@
         def _():
             send(pipe_b, prev_ref, pipe_prev, prev_sent, prev_got)
 
-    wide = width // PARTS_A
-    for part in range(PARTS_A):
+    ret_a.collect_extra()
+    for part, (start, end) in enumerate(parts):
         ret_a.collect(part)
-
-        @pl.loop(0, wide // step)
-        def _(i):
-            cols = pl.ds(pl.multiple_of(part * wide + i * step, step), step)
+        for base in (start, half + start):
+            cols = pl.ds(base, end - start)
             moved = dot(ddt_a[...], ret[:, cols])
             summed = gates_a[0, :, 0:1] * moved[0:tokens] + gates_a[1, :, 0:1] * moved[tokens:]
             pipe_a[:, cols] = (hid_a[:, cols].astype(F32) + summed).astype(BF)
-
-        cols = pl.ds(part * wide, wide)
         if pipes > 1:
             @pl.when(pipe < pipes - 1)
             def _():
-                send(pipe_a.at[:, cols], next_ref.at[:, cols], pipe_next, next_sent, next_got)
+                for base in (start, half + start):
+                    cols = pl.ds(base, end - start)
+                    send(
+                        pipe_a.at[:, cols], next_ref.at[:, cols], pipe_next, next_sent, next_got
+                    )
 
     for ref, sem in unwaited:
         wait_for(ref, sem)
@@ -531,15 +536,28 @@
             wait_for(next_ref, next_got)
 
 
-def hand_over(first, second, first_out, second_out):
-    first_out[...] = first[...]
-    second_out[...] = second[...]
+def hand_over(first, second, first_out, second_out, held, sems):
+    moves = []
+    for n, (source, result) in enumerate(((first, first_out), (second, second_out))):
+        for i in range(2):
+            rows = pl.ds(i * 64, 64)
+            here = held.at[n, rows]
+            moves.append((
+                pltpu.make_async_copy(source.at[rows], here, sems.at[0, n, i]),
+                pltpu.make_async_copy(here, result.at[rows], sems.at[1, n, i]),
+            ))
+    for fetch, _ in moves:
+        fetch.start()
+    for fetch, store in moves:
+        fetch.wait()
+        store.start()
+    for _, store in moves:
+        store.wait()
 
 
 def scratch(tokens, width, ff):
     half = width // 2
     vmem = pltpu.VMEM
-    part = half // PARTS_A
     shapes = [
         ((width, ff), BF), ((width, ff), BF), ((ff, width), BF),
         ((2 * tokens, width), BF), ((2 * tokens, width), BF),
@@ -554,12 +572,13 @@
         ((8, 2, 16, half), BF), ((8, 2, 16, width), BF),
         ((512, width), BF), ((512, width), BF), ((512, width), BF),
         ((512, ff), BF), ((512, ff), BF),
-        ((PARTS_A, 64, 16, part), BF), ((1, 64, 16, half), BF),
-        ((PARTS_A, 16, 16, part), BF), ((1, 16, 16, half), BF),
-        ((7, PARTS_A, 2, 16, part), BF), ((7, 1, 2, 16, half), BF),
-        ((PARTS_A, 2, 16, part), BF), ((1, 2, 16, half), BF),
-        ((PARTS_A, 16, part), BF), ((1, 16, half), BF),
-        ((PARTS_A, 31, 16, part), BF), ((1, 31, 16, half), BF),
+        ((PARTS_A, 32, 16, half // PARTS_A), BF), ((1, 32, 16, half), BF),
+        ((32, 16, half), BF), ((32, 16, half), BF),
+        ((16, 16, half), BF), ((16, 16, half), BF),
+        ((7, 2, 16, half), BF), ((7, 2, 16, half), BF),
+        ((2, 16, half), BF), ((2, 16, half), BF),
+        ((16, half), BF), ((16, half), BF),
+        ((PARTS_A, 31, 16, half // PARTS_A), BF), ((1, 31, 16, half), BF),
         ((384, width), BF), ((tokens, width), F32),
         ((tokens, width), BF), ((tokens, width), BF),
     ]
@@ -582,7 +601,6 @@
         jnp.swapaxes(value[0], 0, 1)
         for value in (expert_ids_a, expert_ids_b, router_probs_a, router_probs_b)
     ]
-    inside = pl.BlockSpec(memory_space=pltpu.VMEM)
     outside = pl.BlockSpec(memory_space=pl.ANY)
     result = jax.ShapeDtypeStruct((tokens, width), BF)
     rows = 512
@@ -605,8 +623,9 @@
     next_hidden, grad_before = pl.pallas_call(
         hand_over,
         out_shape=(result, result),
-        in_specs=[inside] * 2,
-        out_specs=(inside, inside),
+        in_specs=[outside] * 2,
+        out_specs=(outside, outside),
+        scratch_shapes=[pltpu.VMEM((2, tokens, width), BF), pltpu.SemaphoreType.DMA((2, 2, 2))],
     )(next_hidden, grad_before)
     return next_hidden[None], grad_before[None]
 

time: 162 us -> 161 us (level)
  no operation moved by 1% of the time
where the time goes in v3:
time: 161 us
  Pallas kernels  161 us (100%)
    pallas_call x1, Pallas kernels, per_device(): pl.pallas_call(kernel, out_shape=(result, result), in_specs=[outside] * 1...  159 us

profile of v3, /device:TPU:6, one launch (start us, length us, event | category | flops | bytes accessed | tf_op | source)
XLA Modules:
  0.0 161.2 jit_solution(14953848137551932327)
XLA Ops:
  0.6 158.6 %shard_map.122 = (bf16[128,2048]{1,0:T(8,128)(2,1)}, bf16[128,2048]{1,0:T(8,128)(2,1)}) custom-call(s32[8,128]{1,0:T(8,128)} %bitcast.28, s32[8,128]{1,0:T(8,128)} %bitcast.29, f32[8,128]{1,0:T(8,128)} %bitcast.30, f32[8,128]{1,0:T(8,128)} %bitcast.31, bf16[128,2048]{1,0:T(8,128)(2,1)} %bitcast.23, bf16[128,2048]{1,0:T(8,128)(2,1)} %bitcast.24, ...), custom_call_target="tpu_custom_call" | custom-call | flops 12884901888 | bytes 9437184 | tf_op jit(solution)/shard_map/pallas_call | solution.py:607
  159.2 2.0 %shard_map.123 = (bf16[128,2048]{1,0:T(8,128)(2,1)}, bf16[128,2048]{1,0:T(8,128)(2,1)}) custom-call(bf16[128,2048]{1,0:T(8,128)(2,1)} %get-tuple-element.6.first, bf16[128,2048]{1,0:T(8,128)(2,1)} %get-tuple-element.7.second), custom_call_target="tpu_custom_call" | custom-call | tf_op jit(solution)/shard_map/pallas_call | solution.py:623

commit v4 on v3

--- a/solution.py
+++ b/solution.py
@@ -467,11 +467,11 @@
     ret_b.swap()
     ret_b.launch(0, BLOCKS[:8])
     dis_a.collect()
-    ret_b.launch(0, BLOCKS[8:14])
+    ret_b.launch(0, BLOCKS[8:16])
     run(forward_units, 0, tiles)
     run(forward_out, 0, half // TILE)
     ret_a.swap()
-    for h, (start, end) in enumerate(((14, 20), (20, 26), (26, 31), (31, 31))):
+    for h, (start, end) in enumerate(((16, 21), (21, 26), (26, 31), (31, 31))):
         ret_b.extra(h + 1)
         ret_a.extra(h + 1)
         ret_b.launch(0, BLOCKS[start:end])

time: 161 us -> 160 us (level)
  Pallas kernels: 161 us -> 159 us
where the time goes in v4:
time: 160 us
  Pallas kernels  159 us (99%)
    pallas_call x1, Pallas kernels, per_device(): pl.pallas_call(kernel, out_shape=(result, result), in_specs=[outside] * 1...  157 us

profile of v4, /device:TPU:6, one launch (start us, length us, event | category | flops | bytes accessed | tf_op | source)
XLA Modules:
  0.0 159.8 jit_solution(9853601144948669740)
XLA Ops:
  0.6 157.1 %shard_map.122 = (bf16[128,2048]{1,0:T(8,128)(2,1)}, bf16[128,2048]{1,0:T(8,128)(2,1)}) custom-call(s32[8,128]{1,0:T(8,128)} %bitcast.28, s32[8,128]{1,0:T(8,128)} %bitcast.29, f32[8,128]{1,0:T(8,128)} %bitcast.30, f32[8,128]{1,0:T(8,128)} %bitcast.31, bf16[128,2048]{1,0:T(8,128)(2,1)} %bitcast.23, bf16[128,2048]{1,0:T(8,128)(2,1)} %bitcast.24, ...), custom_call_target="tpu_custom_call" | custom-call | flops 12884901888 | bytes 9437184 | tf_op jit(solution)/shard_map/pallas_call | solution.py:607
  157.8 2.0 %shard_map.123 = (bf16[128,2048]{1,0:T(8,128)(2,1)}, bf16[128,2048]{1,0:T(8,128)(2,1)}) custom-call(bf16[128,2048]{1,0:T(8,128)(2,1)} %get-tuple-element.6.first, bf16[128,2048]{1,0:T(8,128)(2,1)} %get-tuple-element.7.second), custom_call_target="tpu_custom_call" | custom-call | tf_op jit(solution)/shard_map/pallas_call | solution.py:623
